TPU v7x, 256 devices: a whole 4x4x8 slice. The times are simulated.
256 devices in a mesh: az: 8 (over y, x_lo), ax: 32 (over z, x_hi, core).
Axes of the slice: x: 4 (x_hi: 2, x_lo: 2; x = x_hi * 2 + x_lo), y: 4, z: 8, core: 2. Of those that a mesh axis runs over, the one named last changes fastest.
Arguments:
- velocity: float32 [3, 512, 64, 256], P(None, 'az', 'ax'), may hold values from -5 to 5
- viscosity: bfloat16 [512, 64, 256], P('az', 'ax'), may hold values from 0.5 to 2
- bfield: bfloat16 [3, 512, 64, 256], P(None, 'az', 'ax'), may hold values from -4 to 4
- particle_velocity: float32 [3, 2097152], P(None, ('az', 'ax')), may hold values from -5 to 5
- particle_cell: int32 [3, 2097152], P(None, ('az', 'ax')), may hold values from 0 to 511, as said below
- send_rows: int32 [256, 8, 128], P(('az', 'ax')), may hold values from 0 to 8191, as said below
- send_counts: int32 [8, 32, 8], P(None, 'ax'), may hold values from 0 to 128, as said below
Outputs:
- new_velocity: float32 [3, 512, 64, 256], P(None, 'az', 'ax')
- kept_velocity: float32 [3, 2097152], P(None, ('az', 'ax'))
- arrival_velocity: float32 [256, 3, 1024], P(('az', 'ax'))
Inputs may be any that keep to these rules, and one draw needn't show every extreme that they name: `send_counts`: zero toward the device's own sector, exactly 128 toward each of the two neighbouring sectors, 0 to 64 toward the others. `send_rows`: within one device's lists all rows are distinct; rows in slots at or beyond the count stay and are ignored for leaving. `particle_cell`: row 0 lies in 0 to 511, row 1 in 0 to 255, row 2 in 0 to 63. A leaving inclusion's cell lies in the target sector, every other in its own device's sector; the axial cell always lies in the device's own slab.
All inputs are finite; a program needn't handle non-finite values.
Results may differ from a plain program's by a relative error of at most 0.0003.
Values sent between devices are 32-bit elements; how exact they have to be, the bound alone decides.
No kernel may reach another device: no remote copies, remote signals or barrier semaphores. Data moves between devices by JAX's collectives and lax.ppermute only.
A program may use at most 128 MiB of HBM per device.

v0:
```python
import math

import jax
import jax.numpy as jnp
import numpy as np
from jax import lax
from jax.experimental import pallas as pl
from jax.experimental.pallas import tpu as pltpu
from jax.sharding import PartitionSpec as P

NA = 512
NR = 256
KR = 32
SECT = 8
TH = NA // SECT
CAP = 128
NP = 8192
DTHETA = 2.0 * math.pi / NA
DT = 0.02
POLE_SIGNS = (-1.0, -1.0, 1.0)
HIGHEST = lax.Precision.HIGHEST
f32 = jnp.float32
bf16 = jnp.bfloat16
i32 = jnp.int32
VMEM_LIMIT = 65408 * 1024

ROW_B = 64
ROW_EDGE = 128
EDGE_PART = 16
EDGE1 = 24
EDGE2 = 16
CHUNK = 2048


def filter_tables():
    a = np.arange(NA // 2)
    even, odd, even_mode, odd_mode = [], [], [], []
    for m in range(NA // 2 + 1):
        scale = math.sqrt((1.0 if m in (0, NA // 2) else 2.0) / NA)
        phase = 2.0 * math.pi * (m * a % NA) / NA
        rows = [scale * np.cos(phase)]
        if m not in (0, NA // 2):
            rows.append(scale * np.sin(phase))
        for row in rows:
            (odd if m % 2 else even).append(row)
            (odd_mode if m % 2 else even_mode).append(m)
    basis = np.stack([np.stack(even), np.stack(odd)]).astype(np.float32)
    modes = np.stack([np.array(even_mode), np.array(odd_mode)]).astype(np.float64)
    cutoff = 4.0 * (np.arange(KR) + 0.5)
    weight = 1.0 / (1.0 + (modes[:, :, None] / cutoff) ** 4)
    weight = np.tile(weight, (1, 1, 256 // KR)).astype(np.float32)
    return basis, np.ascontiguousarray(basis.transpose(0, 2, 1)), weight


BASIS, BASIS_T, MODE_WEIGHT = filter_tables()


def lane_iota(shape):
    return lax.broadcasted_iota(i32, shape, len(shape) - 1)


def row_iota(shape):
    return lax.broadcasted_iota(i32, shape, len(shape) - 2)


def strided(c, z, h):
    return pl.ds(c * 256 + h * 2 + z, TH, stride=4)


def block(c, z, h):
    return pl.ds(((c * 2 + z) * 2 + h) * TH, TH)


def lanes(x, by):
    by %= 128
    return x if by == 0 else pltpu.roll(x, by, 1)


def split2(x):
    hi = x.astype(bf16)
    return hi, (x - hi.astype(f32)).astype(bf16)


def split3(x):
    hi = x.astype(bf16)
    rest = x - hi.astype(f32)
    mid = rest.astype(bf16)
    return hi, mid, (rest - mid.astype(f32)).astype(bf16)


def pack_inner(field, nu):
    lane = lane_iota((TH, 128))

    def four(p, q, r, s):
        low = jnp.where(lane < 32, p, lanes(q, 32))
        high = jnp.where(lane < 96, lanes(r, 64), lanes(s, 96))
        return jnp.where(lane < 64, low, high)

    first = four(field[0][0][0], field[0][1][0], field[1][0][0], field[1][1][0])
    second = four(field[2][0][0], field[2][1][0], nu[0], nu[1])
    return first, second


def write_message(inner_ref, edge_ref, field, nu, me):
    first, second = pack_inner(field, nu)
    inner_ref[0:TH, :] = first
    inner_ref[TH : 2 * TH, :] = second
    up = (me + 1) % SECT
    for c in range(3):
        for z in range(2):
            for h in range(2):
                x = field[c][z][h]
                row = (c * 2 + z) * 2 + h
                for t in range(SECT):
                    edge_ref[t, row : row + 1, :] = jnp.where(t == up, x[TH - 1 : TH], x[0:1])


def send_message(out, edges):
    inner = out.vmem("inner")
    for t in range(SECT):
        out.copy(inner, out.hbm("msg").at[t, 0:ROW_EDGE, :])
    out.copy(edges, out.hbm("msg").at[:, ROW_EDGE:, :])


def write_axial(one_ref, two_ref, field, slab):
    odd = slab % 2 == 1
    for c in range(3):
        for h in range(2):
            rows = pl.ds((c * 2 + h) * TH, TH)
            low, high = field[c][0][h], field[c][1][h]
            one_ref[rows, :] = jnp.where(odd, low, high)
            two_ref[rows, :] = jnp.where(odd, high, low)


class Inputs:
    def __init__(self, names, refs, bufs, sems):
        self.refs = dict(zip(names, bufs))
        self.copies = {}
        for i, (name, ref, buf) in enumerate(zip(names, refs, bufs)):
            if name == "inner":
                ref = ref.at[:, 0:ROW_EDGE, :]
            if name == "edge":
                ref = ref.at[:, ROW_EDGE:, :]
            self.copies[name] = [pltpu.make_async_copy(ref, buf, sems.at[i])]
            self.copies[name][0].start()

    def __call__(self, name):
        for copy in self.copies.pop(name, ()):
            copy.wait()
        return self.refs[name]


class Outputs:
    def __init__(self, names, refs, bufs, sems):
        self.refs, self.bufs, self.sems, self.started = dict(zip(names, refs)), bufs, sems, []

    def hbm(self, name):
        return self.refs[name]

    def vmem(self, name):
        return self.bufs[name]

    def copy(self, src, dst):
        copy = pltpu.make_async_copy(src, dst, self.sems.at[len(self.started)])
        copy.start()
        self.started.append(copy)

    def send(self, name):
        self.copy(self.bufs[name], self.refs[name])

    def finish(self):
        for copy in self.started:
            copy.wait()


def pack_kernel(inp, out):
    me = lax.axis_index("az")
    slab = lax.axis_index("ax")
    pv_ref, pc_ref = inp("pv"), inp("pc")
    tmp_ref, nu_s, edge_ref, stay_ref = out.vmem("tmp"), out.vmem("nu"), out.vmem("edge"), out.vmem("stay")
    for i in range(64):
        tmp_ref[i * 8 : i * 8 + 3, :] = pv_ref[:, i * 128 : (i + 1) * 128]
        tmp_ref[512 + i * 8 : 512 + i * 8 + 3, :] = pc_ref[:, i * 128 : (i + 1) * 128].astype(f32)
    parts = []
    for k in range(2):
        for c in range(3):
            parts.append(split3(tmp_ref[pl.ds(k * 512 + c, 64, stride=8), :]))
    stack = jnp.concatenate([jnp.concatenate([p[s] for p in parts], axis=1) for s in range(3)], axis=0)
    rows_ref, cnt_ref = inp("rows"), inp("cnt")
    high_iota = row_iota((64, 128))
    low_iota = row_iota((128, 128))
    highs, lows, used_lows = [], [], []
    lane = lane_iota((1, 128))
    for t in range(SECT):
        row = rows_ref[0, t : t + 1, :]
        used = (lane < cnt_ref[me, 0, t]).astype(f32)
        highs.append((high_iota == row // 128).astype(f32).astype(bf16))
        low = (low_iota == row % 128).astype(f32)
        lows.append(low)
        used_lows.append((low * used).astype(bf16))
    high = jnp.concatenate(highs, axis=1)
    leaving = lax.dot_general(
        high, jnp.concatenate(used_lows, axis=1), (((1,), (1,)), ((), ())), preferred_element_type=f32
    )
    stay = 1.0 - leaving
    for i in range(64):
        stay_ref[0:1, i * 128 : (i + 1) * 128] = stay[i : i + 1, :]
    out.send("stay")
    picked = lax.dot_general(
        stack, jnp.concatenate([high, high, high], axis=0), (((0,), (0,)), ((), ())), preferred_element_type=f32
    )
    for t in range(SECT):
        for q in range(6):
            value = picked[q * 128 : (q + 1) * 128, t * 128 : (t + 1) * 128] * lows[t]
            edge_ref[t, EDGE_PART + q : EDGE_PART + q + 1, :] = jnp.sum(value, axis=0, keepdims=True)
    vel_ref, nu_ref = inp("vel"), inp("nu")
    field = [[[vel_ref[strided(c, z, h), :] for h in range(2)] for z in range(2)] for c in range(3)]
    nu_s[...] = nu_ref[...].astype(f32)
    nu = [nu_s[pl.ds(z, TH, stride=4), :] for z in range(2)]
    write_message(out.vmem("inner"), edge_ref, field, nu, me)
    send_message(out, edge_ref)
    write_axial(out.vmem("one"), out.vmem("two"), field, slab)
    out.send("one")
    out.send("two")


def local_row(theta, r, z, me, slab):
    return ((z - 2 * slab) * 2 + r // 128) * TH + theta - me * TH


def one_hot_pair(row, col, n):
    rows = (row_iota((256, n)) == row).astype(f32).astype(bf16)
    cols = row_iota((128, n)) == col
    return rows, cols


def deposit(row, col, velocity, n):
    rows, cols = one_hot_pair(row, col, n)
    pieces = []
    for c in range(3):
        for part in split2(velocity[c]):
            pieces.append(jnp.where(cols, part.astype(f32), 0.0).astype(bf16))
    pieces.append(cols.astype(f32).astype(bf16))
    return lax.dot_general(
        rows, jnp.concatenate(pieces, axis=0), (((1,), (1,)), ((), ())), preferred_element_type=f32
    )


def add_deposit(acc):
    out = [acc[:, c * 256 : c * 256 + 128] + acc[:, c * 256 + 128 : c * 256 + 256] for c in range(3)]
    out.append(acc[:, 768:896])
    return out


def scatter_kernel(inp, out):
    me = lax.axis_index("az")
    slab = lax.axis_index("ax")
    pc_ref, stay_ref, pv_ref = inp("pc"), inp("stay"), inp("pv")
    sum_ref, acc_ref = out.vmem("sums"), out.vmem("acc")
    for k in range(NP // CHUNK):
        part = pl.ds(k * CHUNK, CHUNK)
        row = local_row(pc_ref[0:1, part], pc_ref[1:2, part], pc_ref[2:3, part], me, slab)
        row = jnp.where(stay_ref[0:1, part] > 0.5, row, -1)
        col = pc_ref[1:2, part] % 128
        more = deposit(row, col, [pv_ref[c : c + 1, part] for c in range(3)], CHUNK)
        if k == 0:
            acc_ref[...] = more
        else:
            acc_ref[...] += more
    for c, x in enumerate(add_deposit(acc_ref[...])):
        sum_ref[c * 256 : (c + 1) * 256, :] = x
    out.send("sums")


def arrivals(edge_ref, cnt_ref, me, slab):
    lane = lane_iota((1, CAP))
    live = jnp.concatenate([(lane < cnt_ref[s, 0, me]).astype(i32) for s in range(SECT)], axis=1)

    def channel(q):
        return jnp.concatenate([edge_ref[s, EDGE_PART + q : EDGE_PART + q + 1, :] for s in range(SECT)], axis=1)

    velocity = [channel(c) for c in range(3)]
    theta, r, z = [channel(3 + c).astype(i32) for c in range(3)]
    row = jnp.where(live > 0, local_row(theta, r, z, me, slab), -1)
    return live, row, r % 128, velocity


def filtered_inner(inp, me):
    recv_ref = inp("inner")
    first = recv_ref[:, 0:TH, :].reshape(NA, 128)
    second = recv_ref[:, ROW_B : ROW_B + TH, :].reshape(NA, 128)
    lane = lane_iota((1, 128))
    radius = (lane % KR).astype(f32) + 0.5
    left = lane < 64
    first_swap = pltpu.roll(first, 64, 1)
    second_swap = pltpu.roll(second, 64, 1)
    nu = jnp.where(left, second_swap, second)
    swirl = jnp.where(left, first_swap, first)

    def differences(x):
        after = pltpu.roll(x, NA - 1, 0)
        before = pltpu.roll(x, 1, 0)
        lap = (after - 2.0 * x + before) * (1.0 / (radius * radius * (DTHETA * DTHETA)))
        return lap, (after - before) * (1.0 / (2.0 * DTHETA * radius))

    lap, grad = differences(first)
    cross = jnp.where(left, -2.0, 2.0) / radius
    part_first = nu * lap - swirl * grad + cross * nu * pltpu.roll(grad, 64, 1)
    lap, grad = differences(second)
    part_second = jnp.where(left, nu * lap - swirl * grad, 0.0)
    part = jnp.concatenate([part_first, part_second], axis=1)
    low, high = part[: NA // 2], part[NA // 2 :]
    basis_ref, weight_ref, basis_t_ref = inp("basis"), inp("weight"), inp("basis_t")
    own = pl.ds(pl.multiple_of((me % 4) * TH, TH), TH)
    out = 0.0
    for parity, x in enumerate((low + high, low - high)):
        spectrum = jnp.dot(basis_ref[parity], x, precision=HIGHEST, preferred_element_type=f32)
        spectrum = spectrum * weight_ref[parity]
        back = jnp.dot(basis_t_ref[parity, own, :], spectrum, precision=HIGHEST, preferred_element_type=f32)
        if parity:
            back = jnp.where(me < 4, back, -back)
        out = out + back
    return out[:, :128], out[:, 128:]


def fluid_rate(field, nu, magnetic, inp, me, slab):
    filtered = filtered_inner(inp, me)
    recv_ref, edge_ref, one_ref, two_ref = inp("inner"), inp("edge"), inp("one"), inp("two")
    odd = slab % 2 == 1
    before_sector = (me + SECT - 1) % SECT
    after_sector = (me + 1) % SECT
    opposite = (me + SECT // 2) % SECT
    lane = lane_iota((TH, 128))
    row = row_iota((TH, 128))
    poles = [recv_ref[opposite, 0:TH, :], recv_ref[opposite, ROW_B : ROW_B + TH, :]]
    rates = [[[None, None], [None, None]] for _ in range(3)]
    for z in range(2):
        ghosts = []
        for c in range(3):
            ghosts.append(POLE_SIGNS[c] * lanes(poles[c // 2], -((c % 2) * 64 + z * 32)))
        rolled = [[(pltpu.roll(field[c][z][h], 1, 1), pltpu.roll(field[c][z][h], 127, 1)) for h in range(2)] for c in range(3)]
        for h in range(2):
            radius = lane_iota((1, 128)).astype(f32) + (h * 128 + 0.5)
            inverse = 1.0 / radius
            eddy = nu[z][h]
            u = [field[c][z][h] for c in range(3)]
            lap_ax, lap_rad, grad_rad, grad_ax, lap_th, grad_th = [], [], [], [], [], []
            for c in range(3):
                x = u[c]
                if h == 0:
                    prev_r = jnp.where(lane == 0, ghosts[c], rolled[c][0][0])
                    next_r = jnp.where(lane == 127, rolled[c][1][1], rolled[c][0][1])
                else:
                    prev_r = jnp.where(lane == 0, rolled[c][0][0], rolled[c][1][0])
                    next_r = jnp.where(lane == 127, 0.0, rolled[c][1][1])
                face = pl.ds((c * 2 + h) * TH, TH)
                if z == 0:
                    prev_z = jnp.where(odd, one_ref[face, :], two_ref[face, :])
                    next_z = field[c][1][h]
                else:
                    prev_z = field[c][0][h]
                    next_z = jnp.where(odd, two_ref[face, :], one_ref[face, :])
                halo = (c * 2 + z) * 2 + h
                prev_t = jnp.where(row == 0, edge_ref[before_sector, halo : halo + 1, :], pltpu.roll(x, 1, 0))
                next_t = jnp.where(row == TH - 1, edge_ref[after_sector, halo : halo + 1, :], pltpu.roll(x, TH - 1, 0))
                lap_rad.append(((radius + 0.5) * (next_r - x) - (radius - 0.5) * (x - prev_r)) * inverse)
                lap_ax.append(next_z - 2.0 * x + prev_z)
                grad_rad.append(0.5 * (next_r - prev_r))
                grad_ax.append(0.5 * (next_z - prev_z))
                lap_th.append((next_t - 2.0 * x + prev_t) * (1.0 / (radius * radius * (DTHETA * DTHETA))))
                grad_th.append((next_t - prev_t) * (1.0 / (2.0 * DTHETA * radius)))
            b = [magnetic[c][z][h] for c in range(3)]
            slip = [-u[0], radius * (2.0 / NR) - u[1], -u[2]]
            current = [slip[1] * b[2] - slip[2] * b[1], slip[2] * b[0] - slip[0] * b[2], slip[0] * b[1] - slip[1] * b[0]]
            force = [
                current[1] * b[2] - current[2] * b[1],
                current[2] * b[0] - current[0] * b[2],
                current[0] * b[1] - current[1] * b[0],
            ]
            inverse2 = inverse * inverse
            metric = [
                u[1] * u[1] * inverse - eddy * u[0] * inverse2,
                -eddy * u[1] * inverse2 - u[0] * u[1] * inverse,
                0.0,
            ]
            coupling = [-2.0 * eddy * grad_th[1] * inverse, 2.0 * eddy * grad_th[0] * inverse, 0.0]
            for c in range(3):
                azimuth = eddy * lap_th[c] - u[1] * grad_th[c] + coupling[c]
                if h == 0:
                    inner = lanes(filtered[c // 2], -((c % 2) * 64 + z * 32))
                    azimuth = jnp.where(lane < KR, inner, azimuth)
                rates[c][z][h] = (
                    eddy * (lap_rad[c] + lap_ax[c])
                    - (u[0] * grad_rad[c] + u[2] * grad_ax[c])
                    + metric[c]
                    + 0.5 * force[c]
                    + azimuth
                )
    return rates


def materials(inp, out):
    nu_s, mag_s = out.vmem("nu"), out.vmem("mag")
    nu_s[...] = inp("nu")[...].astype(f32)
    mag_s[...] = inp("mag")[...].astype(f32)
    nu = [[nu_s[strided(0, z, h), :] for h in range(2)] for z in range(2)]
    magnetic = [[[mag_s[strided(c, z, h), :] for h in range(2)] for z in range(2)] for c in range(3)]
    return nu, magnetic


def first_kernel(inp, out):
    me = lax.axis_index("az")
    slab = lax.axis_index("ax")
    live, row, col, velocity = arrivals(inp("edge"), inp("cnt"), me, slab)
    arrived = add_deposit(deposit(row, col, velocity, SECT * CAP))
    sum_ref = inp("sums")
    total = [sum_ref[c * 256 : (c + 1) * 256, :] + arrived[c] for c in range(4)]
    nu, magnetic = materials(inp, out)
    vel_ref = inp("vel")
    field = [[[vel_ref[strided(c, z, h), :] for h in range(2)] for z in range(2)] for c in range(3)]
    rates = fluid_rate(field, nu, magnetic, inp, me, slab)
    mid_ref, rest_ref, pick_ref = out.vmem("mid"), out.vmem("rest"), out.vmem("pick")
    mid = [[[None, None], [None, None]] for _ in range(3)]
    picks = []
    for c in range(3):
        halves = []
        for z in range(2):
            for h in range(2):
                at = slice((z * 2 + h) * TH, (z * 2 + h + 1) * TH)
                x, s, n = field[c][z][h], total[c][at], total[3][at]
                u1 = x + DT * (rates[c][z][h] + 2.0 * (s - n * x))
                mid[c][z][h] = u1
                mid_ref[block(c, z, h), :] = u1
                rest_ref[block(c, z, h), :] = 0.5 * (x + u1) + DT * (0.8 * s + 0.2 * n * x - n * u1)
                halves.append(0.08 * x + 0.1 * u1)
        picks.append(jnp.concatenate(halves, axis=0))
    write_message(out.vmem("inner"), out.vmem("edge"), mid, [nu[z][0] for z in range(2)], me)
    send_message(out, out.vmem("edge"))
    write_axial(out.vmem("one"), out.vmem("two"), mid, slab)
    out.send("one")
    out.send("two")
    out.send("mid")
    out.send("rest")
    for c in range(3):
        hi, lo = split2(picks[c].T)
        pick_ref[c * 128 : (c + 1) * 128, 0:256] = hi
        pick_ref[c * 128 : (c + 1) * 128, 256:512] = lo
    out.send("pick")


def take(pick, row, col, n):
    rows, cols = one_hot_pair(row, col, n)
    got = jnp.dot(pick, jnp.concatenate([rows, rows], axis=0), preferred_element_type=f32)
    return [jnp.sum(jnp.where(cols, got[c * 128 : (c + 1) * 128], 0.0), axis=0, keepdims=True) for c in range(3)]


def gather_kernel(inp, out):
    me = lax.axis_index("az")
    slab = lax.axis_index("ax")
    pc_ref, stay_ref, pv_ref = inp("pc"), inp("stay"), inp("pv")
    kept_ref, arr_ref = out.vmem("kept"), out.vmem("arrived")
    pick = inp("pick")[...]
    for k in range(NP // CHUNK):
        part = pl.ds(k * CHUNK, CHUNK)
        row = local_row(pc_ref[0:1, part], pc_ref[1:2, part], pc_ref[2:3, part], me, slab)
        stay = stay_ref[0:1, part] > 0.5
        row = jnp.where(stay, row, -1)
        got = take(pick, row, pc_ref[1:2, part] % 128, CHUNK)
        for c in range(3):
            kept_ref[c : c + 1, part] = jnp.where(stay, 0.82 * pv_ref[c : c + 1, part] + got[c], 0.0)
    out.send("kept")
    live, row, col, velocity = arrivals(inp("edge"), inp("cnt"), me, slab)
    got = take(pick, row, col, SECT * CAP)
    for c in range(3):
        arr_ref[c, 0:1, :] = jnp.where(live > 0, 0.82 * velocity[c] + got[c], 0.0)
    out.send("arrived")


def last_kernel(inp, out):
    me = lax.axis_index("az")
    slab = lax.axis_index("ax")
    mid_ref = inp("mid")
    field = [[[mid_ref[block(c, z, h), :] for h in range(2)] for z in range(2)] for c in range(3)]
    nu, magnetic = materials(inp, out)
    rates = fluid_rate(field, nu, magnetic, inp, me, slab)
    rest_ref, out_ref = inp("rest"), out.vmem("new")
    for c in range(3):
        for z in range(2):
            for h in range(2):
                out_ref[strided(c, z, h), :] = rest_ref[block(c, z, h), :] + (0.5 * DT) * rates[c][z][h]
    out.send("new")


def call(kernel, name, ins, outs, bufs, copies, flops=0, in_smem=()):
    in_names, out_names, buf_names = list(ins), list(outs), list(bufs)
    arrays = [ins[n] for n in in_names]
    n_in, n_out = len(in_names), len(out_names)

    def body(*refs):
        in_refs, refs = refs[:n_in], refs[n_in:]
        out_refs, refs = refs[:n_out], refs[n_out:]
        in_bufs, refs = refs[:n_in], refs[n_in:]
        buf_refs, (in_sems, out_sems) = refs[:-2], refs[-2:]
        out = Outputs(out_names, out_refs, dict(zip(buf_names, buf_refs)), out_sems)
        kernel(Inputs(in_names, in_refs, in_bufs, in_sems), out)
        out.finish()

    def in_shape(n):
        shape = ins[n].shape
        return {"inner": (SECT, ROW_EDGE, 128), "edge": (SECT, shape[1] - ROW_EDGE, 128)}.get(n, shape)

    hbm = pl.BlockSpec(memory_space=pltpu.HBM)
    return pl.pallas_call(
        body,
        out_shape=[jax.ShapeDtypeStruct(*outs[n]) for n in out_names],
        in_specs=[hbm] * n_in,
        out_specs=[hbm] * n_out,
        scratch_shapes=[(pltpu.SMEM if n in in_smem else pltpu.VMEM)(in_shape(n), ins[n].dtype) for n in in_names]
        + [pltpu.VMEM(*bufs[n]) for n in buf_names]
        + [pltpu.SemaphoreType.DMA((n_in,)), pltpu.SemaphoreType.DMA((copies,))],
        compiler_params=pltpu.CompilerParams(vmem_limit_bytes=VMEM_LIMIT),
        cost_estimate=pl.CostEstimate(flops=flops, bytes_accessed=2 * 1024 * 1024, transcendentals=0),
        name=name,
    )(*arrays)


def rows_of(x):
    lead = x.shape[:-2]
    x = x.reshape(*lead, 2, 2, 128)
    return jnp.swapaxes(x, -3, -2).reshape(-1, 128)


def per_device(velocity, viscosity, bfield, particle_velocity, particle_cell, send_rows, send_counts):
    ax = lax.axis_size("ax")
    vel, nu, mag = rows_of(velocity), rows_of(viscosity), rows_of(bfield)
    pv, pc = particle_velocity, particle_cell
    tables = {"basis": jnp.asarray(BASIS), "weight": jnp.asarray(MODE_WEIGHT), "basis_t": jnp.asarray(BASIS_T)}
    swap_one = [(i, i ^ 1) for i in range(ax)]
    swap_two = [(i, ((i + 1) ^ 1) - 1) for i in range(1, ax - 1)]

    def exchange(msg, one, two):
        one = lax.ppermute(one, "ax", swap_one)
        two = lax.ppermute(two, "ax", swap_two)
        return lax.all_to_all(msg, "az", split_axis=0, concat_axis=0, tiled=True), one, two

    face = ((384, 128), f32)
    field = ((768, 128), f32)
    materials_bufs = {"nu": ((256, 128), f32), "mag": field}
    message_bufs = {"inner": ((ROW_EDGE, 128), f32), "one": face, "two": face}
    msg, one, two, stay = call(
        pack_kernel,
        "pack",
        {"pc": pc, "pv": pv, "rows": send_rows, "cnt": send_counts, "vel": vel, "nu": nu},
        {"msg": ((SECT, ROW_EDGE + EDGE1, 128), f32), "one": face, "two": face, "stay": ((1, NP), f32)},
        message_bufs
        | {"edge": ((SECT, EDGE1, 128), f32), "stay": ((1, NP), f32), "tmp": ((1024, 128), f32), "nu": ((256, 128), f32)},
        12,
        in_smem=("cnt",),
    )
    recv, one, two = exchange(msg, one, two)
    (sums,) = call(
        scatter_kernel,
        "deposit",
        {"pc": pc, "stay": stay, "pv": pv},
        {"sums": ((1024, 128), f32)},
        {"sums": ((1024, 128), f32), "acc": ((256, 896), f32)},
        1,
        flops=2 * NP * 256 * 896,
    )
    msg2, one2, two2, mid, rest, pick = call(
        first_kernel,
        "first_section",
        {"edge": recv, "cnt": send_counts, "inner": recv, "sums": sums, "nu": nu, "mag": mag, "vel": vel}
        | tables
        | {"one": one, "two": two},
        {
            "msg": ((SECT, ROW_EDGE + EDGE2, 128), f32),
            "one": face,
            "two": face,
            "mid": field,
            "rest": field,
            "pick": ((384, 512), bf16),
        },
        message_bufs
        | materials_bufs
        | {"edge": ((SECT, EDGE2, 128), f32), "mid": field, "rest": field, "pick": ((384, 512), bf16)},
        14,
        in_smem=("cnt",),
    )
    recv2, one2, two2 = exchange(msg2, one2, two2)
    kept, arrived = call(
        gather_kernel,
        "take",
        {"pc": pc, "stay": stay, "pick": pick, "pv": pv, "edge": recv, "cnt": send_counts},
        {"kept": ((3, NP), f32), "arrived": ((3, 1, SECT * CAP), f32)},
        {"kept": ((3, NP), f32), "arrived": ((3, 1, SECT * CAP), f32)},
        2,
        flops=2 * NP * 512 * 384,
        in_smem=("cnt",),
    )
    (new,) = call(
        last_kernel,
        "second_section",
        {"mid": mid, "inner": recv2, "nu": nu, "mag": mag} | tables | {"edge": recv2, "one": one2, "two": two2, "rest": rest},
        {"new": field},
        materials_bufs | {"new": field},
        1,
    )
    new = jnp.swapaxes(new.reshape(3, TH, 2, 2, 128), 2, 3).reshape(3, TH, 2, NR)
    return new, kept, jnp.swapaxes(arrived, 0, 1)


def solution(mesh):
    return jax.shard_map(
        per_device,
        mesh=mesh,
        in_specs=(
            P(None, "az", "ax", None),
            P("az", "ax", None),
            P(None, "az", "ax", None),
            P(None, ("az", "ax")),
            P(None, ("az", "ax")),
            P(("az", "ax"), None, None),
            P(None, "ax", None),
        ),
        out_specs=(P(None, "az", "ax", None), P(None, ("az", "ax")), P(("az", "ax"), None, None)),
        check_vma=False,
    )
```

profile of v0, /device:TPU:128, one launch (start us, length us, event | category | flops | bytes accessed | tf_op | source)
XLA Modules:
  0.0 53.0 jit_solution(12700218252926011615)
XLA Ops:
  0.6 3.0 %pack.1 = (f32[8,152,128]{2,1,0:T(8,128)}, f32[384,128]{1,0:T(8,128)}, f32[384,128]{1,0:T(8,128)}, f32[1,8192]{1,0:T(1,128)}) custom-call(s32[3,8192]{1,0:T(4,128)} %refs_0_.5, f32[3,8192]{1,0:T(4,128)} %refs_3_.3, s32[1,8,128]{2,1,0:T(8,128)} %refs_2_.2, s32[8,1,8]{2,1,0:T(1,128)} %refs_5_.2, f32[768,128]{1,0:T(8,128)} %bitcast.21, bf16[256,128]{1,0:T(8,128)(2,1)} %bitcast.25), custom_call_target="tpu_custom_call" | custom-call | bytes 2097152 | tf_op jit(solution)/shard_map/pack/pallas_call | solution.py:513
  3.6 5.4 %all-to-all-start = ((f32[8,152,128]{2,1,0:T(8,128)}), f32[8,152,128]{2,1,0:T(8,128)}, u32[]{:S(2)}, u32[]{:S(2)}) async-start(f32[8,152,128]{2,1,0:T(8,128)} %get-tuple-element.15), calls=%async_computation | async-start | bytes 1245184 | tf_op jit(solution)/shard_map/all_to_all | solution.py:544
  9.0 0.0 collective-permute-start
  9.1 4.3 %collective-permute-start.1 = (f32[384,128]{1,0:T(8,128)}, f32[384,128]{1,0:T(8,128)}, u32[]{:S(2)}, u32[]{:S(2)}) collective-permute-start(f32[384,128]{1,0:T(8,128)} %get-tuple-element.18), channel_id=1, source_target_pairs={{1,2},{2,1},{3,4},{4,3},{5,6},{6,5},{7,8},{8,7},{9,10},{10,9},{11,... | collective-permute-start | bytes 589832 | tf_op jit(solution)/shard_map/ppermute | solution.py:543
  13.3 6.3 %deposit.1.refs_3_ = f32[1024,128]{1,0:T(8,128)} custom-call(s32[3,8192]{1,0:T(4,128)} %refs_0_.5, f32[1,8192]{1,0:T(1,128)} %get-tuple-element.16.refs_1_, f32[3,8192]{1,0:T(4,128)} %refs_3_.3), custom_call_target="tpu_custom_call" | custom-call | flops 3758096384 | bytes 2097152 | tf_op jit(solution)/shard_map/deposit/pallas_call | solution.py:513
  19.7 0.0 collective-permute-done.refs_10_
  19.7 0.4 collective-permute-done.1.refs_11_
  20.1 3.8 %all-to-all-done.refs_0_.refs_2_.refs_4_ = f32[8,152,128]{2,1,0:T(8,128)} async-done(((f32[8,152,128]{2,1,0:T(8,128)}), f32[8,152,128]{2,1,0:T(8,128)}, u32[]{:S(2)}, u32[]{:S(2)}) %all-to-all-start) | async-done | bytes 622624 | tf_op jit(solution)/shard_map/all_to_all | solution.py:544
  23.9 5.9 %first_section.1 = (f32[8,144,128]{2,1,0:T(8,128)}, f32[384,128]{1,0:T(8,128)}, f32[384,128]{1,0:T(8,128)}, f32[768,128]{1,0:T(8,128)}, f32[768,128]{1,0:T(8,128)}, /*index=5*/bf16[384,512]{1,0:T(8,128)(2,1)}) custom-call(f32[8,152,128]{2,1,0:T(8,128)} %all-to-all-done.refs_0_.refs_2_.refs_4_, s32[8,1,8]{2,1,0:T(1,128)} %refs_5_.2, ...), custom_call_target="tpu_custom_call" | custom-call | bytes 2097152 | tf_op jit(solution)/shard_map/first_section/pallas_call | solution.py:513
  29.8 4.2 %all-to-all-start.1 = ((f32[8,144,128]{2,1,0:T(8,128)}), f32[8,144,128]{2,1,0:T(8,128)}, u32[]{:S(2)}, u32[]{:S(2)}) async-start(f32[8,144,128]{2,1,0:T(8,128)} %get-tuple-element.20), calls=%async_computation.1 | async-start | bytes 1179648 | tf_op jit(solution)/shard_map/all_to_all | solution.py:544
  34.0 0.1 collective-permute-start.2
  34.1 3.8 %collective-permute-start.3 = (f32[384,128]{1,0:T(8,128)}, f32[384,128]{1,0:T(8,128)}, u32[]{:S(2)}, u32[]{:S(2)}) collective-permute-start(f32[384,128]{1,0:T(8,128)} %get-tuple-element.22), channel_id=1, source_target_pairs={{1,2},{2,1},{3,4},{4,3},{5,6},{6,5},{7,8},{8,7},{9,10},{10,9},{11,... | collective-permute-start | bytes 589832 | tf_op jit(solution)/shard_map/ppermute | solution.py:543
  37.9 7.1 %take.1 = (f32[3,8192]{1,0:T(4,128)}, f32[3,1,1024]{2,1,0:T(1,128)}) custom-call(s32[3,8192]{1,0:T(4,128)} %refs_0_.5, f32[1,8192]{1,0:T(1,128)} %get-tuple-element.16.refs_1_, bf16[384,512]{1,0:T(8,128)(2,1)} %get-tuple-element.24.refs_2_, f32[3,8192]{1,0:T(4,128)} %refs_3_.3, f32[8,152,128]{2,1,0:T(8,128)} %all-to-all-done.refs_0_.refs_2_.refs_4_, ...), custom_call_target="tpu_custom_call" | custom-call | flops 3221225472 | bytes 2097152 | tf_op jit(solution)/shard_map/take/pallas_call | solution.py:513
  45.0 0.0 collective-permute-done.2.refs_8_
  45.0 0.1 collective-permute-done.3.refs_9_
  45.1 3.2 %all-to-all-done.1.refs_1_.refs_7_ = f32[8,144,128]{2,1,0:T(8,128)} async-done(((f32[8,144,128]{2,1,0:T(8,128)}), f32[8,144,128]{2,1,0:T(8,128)}, u32[]{:S(2)}, u32[]{:S(2)}) %all-to-all-start.1) | async-done | bytes 589856 | tf_op jit(solution)/shard_map/all_to_all | solution.py:544
  48.3 4.5 %second_section.1 = f32[768,128]{1,0:T(8,128)} custom-call(f32[768,128]{1,0:T(8,128)} %get-tuple-element.19.refs_0_, f32[8,144,128]{2,1,0:T(8,128)} %all-to-all-done.1.refs_1_.refs_7_, bf16[256,128]{1,0:T(8,128)(2,1)} %bitcast.27, bf16[768,128]{1,0:T(8,128)(2,1)} %bitcast.24, f32[2,256,256]{2,1,0:T(8,128)} %constant.6.clone.refs_7_.refs_4_, ...), custom_call_target="tpu_custom_call" | custom-call | bytes 2097152 | tf_op jit(solution)/shard_map/second_section/pallas_call | solution.py:513
Async XLA Ops:
  3.6 20.2 %all-to-all-start = ((f32[8,152,128]{2,1,0:T(8,128)}), f32[8,152,128]{2,1,0:T(8,128)}, u32[]{:S(2)}, u32[]{:S(2)}) async-start(f32[8,152,128]{2,1,0:T(8,128)} %get-tuple-element.15), calls=%async_computation | async-start | bytes 1245184 | tf_op jit(solution)/shard_map/all_to_all | solution.py:544
  9.0 10.6 %collective-permute-start = (f32[384,128]{1,0:T(8,128)}, f32[384,128]{1,0:T(8,128)}, u32[]{:S(2)}, u32[]{:S(2)}) collective-permute-start(f32[384,128]{1,0:T(8,128)} %get-tuple-element.17), channel_id=1, source_target_pairs={{0,1},{1,0},{2,3},{3,2},{4,5},{5,4},{6,7},{7,6},{8,9},{9,8},{10,11... | collective-permute-start | bytes 589832 | tf_op jit(solution)/shard_map/ppermute | solution.py:542
  9.1 11.0 %collective-permute-start.1 = (f32[384,128]{1,0:T(8,128)}, f32[384,128]{1,0:T(8,128)}, u32[]{:S(2)}, u32[]{:S(2)}) collective-permute-start(f32[384,128]{1,0:T(8,128)} %get-tuple-element.18), channel_id=1, source_target_pairs={{1,2},{2,1},{3,4},{4,3},{5,6},{6,5},{7,8},{8,7},{9,10},{10,9},{11,... | collective-permute-start | bytes 589832 | tf_op jit(solution)/shard_map/ppermute | solution.py:543
  29.8 18.6 %all-to-all-start.1 = ((f32[8,144,128]{2,1,0:T(8,128)}), f32[8,144,128]{2,1,0:T(8,128)}, u32[]{:S(2)}, u32[]{:S(2)}) async-start(f32[8,144,128]{2,1,0:T(8,128)} %get-tuple-element.20), calls=%async_computation.1 | async-start | bytes 1179648 | tf_op jit(solution)/shard_map/all_to_all | solution.py:544
  34.0 11.0 %collective-permute-start.2 = (f32[384,128]{1,0:T(8,128)}, f32[384,128]{1,0:T(8,128)}, u32[]{:S(2)}, u32[]{:S(2)}) collective-permute-start(f32[384,128]{1,0:T(8,128)} %get-tuple-element.21), channel_id=1, source_target_pairs={{0,1},{1,0},{2,3},{3,2},{4,5},{5,4},{6,7},{7,6},{8,9},{9,8},{10,11... | collective-permute-start | bytes 589832 | tf_op jit(solution)/shard_map/ppermute | solution.py:542
  34.1 11.0 %collective-permute-start.3 = (f32[384,128]{1,0:T(8,128)}, f32[384,128]{1,0:T(8,128)}, u32[]{:S(2)}, u32[]{:S(2)}) collective-permute-start(f32[384,128]{1,0:T(8,128)} %get-tuple-element.22), channel_id=1, source_target_pairs={{1,2},{2,1},{3,4},{4,3},{5,6},{6,5},{7,8},{8,7},{9,10},{10,9},{11,... | collective-permute-start | bytes 589832 | tf_op jit(solution)/shard_map/ppermute | solution.py:543
where the time goes:
time: 53.4 us; the launch traced here: 53 us
  Pallas kernels  26.9 us (50%)
  starting transfers between devices  17.8 us (33%)
  waiting for transfers between devices  7.47 us (14%)
  between operations  0.88 us (2%)
    pallas_call x5, Pallas kernels, call(): pl.pallas_call(body, out_shape=[jax.ShapeDtypeStruct(*outs[n]) for n in o...  26.9 us
    all_to_all x2, starting transfers between devices, exchange(): lax.all_to_all(msg, 'az', split_axis=0, concat_axis=0, tiled=True)  9.62 us
    ppermute x2, starting transfers between devices, exchange(): two = lax.ppermute(two, 'ax', swap_two)  8.05 us
    all_to_all x2, waiting for transfers between devices, exchange(): lax.all_to_all(msg, 'az', split_axis=0, concat_axis=0, tiled=True)  7 us
  transfers between devices with their start and end apart: 6, of which 4 were waited for; matrix products, arithmetic and copies ran while one was open for 0% of the time, Pallas kernels for 25%

commit v1 on v0

--- a/solution.py
+++ b/solution.py
@@ -25,11 +25,12 @@
 VMEM_LIMIT = 65408 * 1024
 
 ROW_B = 64
-ROW_EDGE = 128
+ROW_EDGE1 = 128
+ROW_EDGE2 = 96
 EDGE_PART = 16
 EDGE1 = 24
 EDGE2 = 16
-CHUNK = 2048
+CHUNK = 1024
 
 
 def filter_tables():
@@ -48,7 +49,7 @@
     modes = np.stack([np.array(even_mode), np.array(odd_mode)]).astype(np.float64)
     cutoff = 4.0 * (np.arange(KR) + 0.5)
     weight = 1.0 / (1.0 + (modes[:, :, None] / cutoff) ** 4)
-    weight = np.tile(weight, (1, 1, 256 // KR)).astype(np.float32)
+    weight = np.tile(weight, (1, 1, 128 // KR)).astype(np.float32)
     return basis, np.ascontiguousarray(basis.transpose(0, 2, 1)), weight
 
 
@@ -101,10 +102,7 @@
     return first, second
 
 
-def write_message(inner_ref, edge_ref, field, nu, me):
-    first, second = pack_inner(field, nu)
-    inner_ref[0:TH, :] = first
-    inner_ref[TH : 2 * TH, :] = second
+def write_edges(edge_ref, field, me):
     up = (me + 1) % SECT
     for c in range(3):
         for z in range(2):
@@ -115,11 +113,9 @@
                     edge_ref[t, row : row + 1, :] = jnp.where(t == up, x[TH - 1 : TH], x[0:1])
 
 
-def send_message(out, edges):
-    inner = out.vmem("inner")
+def send_inner(out, rows):
     for t in range(SECT):
-        out.copy(inner, out.hbm("msg").at[t, 0:ROW_EDGE, :])
-    out.copy(edges, out.hbm("msg").at[:, ROW_EDGE:, :])
+        out.copy(out.vmem("inner"), out.hbm("msg").at[t, 0:rows, :])
 
 
 def write_axial(one_ref, two_ref, field, slab):
@@ -132,15 +128,21 @@
             two_ref[rows, :] = jnp.where(odd, high, low)
 
 
+def message_rows(name, rows):
+    edge = ROW_EDGE1 if rows == ROW_EDGE1 + EDGE1 else ROW_EDGE2
+    return {"inner": slice(0, edge), "edge": slice(edge, rows), "inner_nu": slice(ROW_B, edge)}[name]
+
+
 class Inputs:
     def __init__(self, names, refs, bufs, sems):
         self.refs = dict(zip(names, bufs))
         self.copies = {}
         for i, (name, ref, buf) in enumerate(zip(names, refs, bufs)):
-            if name == "inner":
-                ref = ref.at[:, 0:ROW_EDGE, :]
-            if name == "edge":
-                ref = ref.at[:, ROW_EDGE:, :]
+            if name in ("inner", "edge", "inner_nu"):
+                ref = ref.at[:, message_rows(name, ref.shape[1]), :]
+            if name == "basis_t":
+                own = lax.axis_index("az") % 4
+                ref = ref.at[:, pl.ds(pl.multiple_of(own * TH, TH), TH), :]
             self.copies[name] = [pltpu.make_async_copy(ref, buf, sems.at[i])]
             self.copies[name][0].start()
 
@@ -175,9 +177,19 @@
 
 def pack_kernel(inp, out):
     me = lax.axis_index("az")
-    slab = lax.axis_index("ax")
+    tmp_ref, nu_s, edge_ref, stay_ref = out.vmem("tmp"), out.vmem("nu"), out.vmem("edge"), out.vmem("stay")
+    vel_ref, nu_ref = inp("vel"), inp("nu")
+    field = [[[vel_ref[strided(c, z, h), :] for h in range(2)] for z in range(2)] for c in range(3)]
+    nu_s[...] = nu_ref[...].astype(f32)
+    nu = [nu_s[pl.ds(z, TH, stride=4), :] for z in range(2)]
+    inner_ref = out.vmem("inner")
+    inner_ref[0:TH, :], inner_ref[TH:, :] = pack_inner(field, nu)
+    send_inner(out, ROW_EDGE1)
+    write_axial(out.vmem("one"), out.vmem("two"), field, lax.axis_index("ax"))
+    out.send("one")
+    out.send("two")
+    write_edges(edge_ref, field, me)
     pv_ref, pc_ref = inp("pv"), inp("pc")
-    tmp_ref, nu_s, edge_ref, stay_ref = out.vmem("tmp"), out.vmem("nu"), out.vmem("edge"), out.vmem("stay")
     for i in range(64):
         tmp_ref[i * 8 : i * 8 + 3, :] = pv_ref[:, i * 128 : (i + 1) * 128]
         tmp_ref[512 + i * 8 : 512 + i * 8 + 3, :] = pc_ref[:, i * 128 : (i + 1) * 128].astype(f32)
@@ -213,43 +225,49 @@
         for q in range(6):
             value = picked[q * 128 : (q + 1) * 128, t * 128 : (t + 1) * 128] * lows[t]
             edge_ref[t, EDGE_PART + q : EDGE_PART + q + 1, :] = jnp.sum(value, axis=0, keepdims=True)
-    vel_ref, nu_ref = inp("vel"), inp("nu")
-    field = [[[vel_ref[strided(c, z, h), :] for h in range(2)] for z in range(2)] for c in range(3)]
-    nu_s[...] = nu_ref[...].astype(f32)
-    nu = [nu_s[pl.ds(z, TH, stride=4), :] for z in range(2)]
-    write_message(out.vmem("inner"), edge_ref, field, nu, me)
-    send_message(out, edge_ref)
-    write_axial(out.vmem("one"), out.vmem("two"), field, slab)
-    out.send("one")
-    out.send("two")
+    out.copy(edge_ref, out.hbm("msg").at[:, ROW_EDGE1:, :])
 
 
 def local_row(theta, r, z, me, slab):
     return ((z - 2 * slab) * 2 + r // 128) * TH + theta - me * TH
 
 
-def one_hot_pair(row, col, n):
-    rows = (row_iota((256, n)) == row).astype(f32).astype(bf16)
-    cols = row_iota((128, n)) == col
-    return rows, cols
+def spread(x, rows, n):
+    tile = jnp.broadcast_to(x, (16, n)).astype(bf16)
+    return jnp.concatenate([tile] * (rows // 16), axis=0)
+
+
+def matches(index, rows, n):
+    return row_iota((rows, n)).astype(f32).astype(bf16) == spread(index.astype(f32), rows, n)
+
+
+def one_hot(index, rows, n):
+    return jnp.where(matches(index, rows, n), jnp.ones((), bf16), jnp.zeros((), bf16))
 
 
 def deposit(row, col, velocity, n):
-    rows, cols = one_hot_pair(row, col, n)
+    cols = matches(col, 128, n)
     pieces = []
     for c in range(3):
         for part in split2(velocity[c]):
-            pieces.append(jnp.where(cols, part.astype(f32), 0.0).astype(bf16))
-    pieces.append(cols.astype(f32).astype(bf16))
+            pieces.append(jnp.where(cols, spread(part.astype(f32), 128, n), jnp.zeros((), bf16)))
+    pieces.append(one_hot(col, 128, n))
     return lax.dot_general(
-        rows, jnp.concatenate(pieces, axis=0), (((1,), (1,)), ((), ())), preferred_element_type=f32
-    )
-
-
-def add_deposit(acc):
+        one_hot(row, 256, n), jnp.concatenate(pieces, axis=0), (((1,), (1,)), ((), ())), preferred_element_type=f32
+    )
+
+
+def add_parts(acc):
     out = [acc[:, c * 256 : c * 256 + 128] + acc[:, c * 256 + 128 : c * 256 + 256] for c in range(3)]
     out.append(acc[:, 768:896])
     return out
+
+
+def write_blocks(ref, x):
+    for c in range(3):
+        for z in range(2):
+            for h in range(2):
+                ref[block(c, z, h), :] = x[c][z][h]
 
 
 def scatter_kernel(inp, out):
@@ -267,9 +285,12 @@
             acc_ref[...] = more
         else:
             acc_ref[...] += more
-    for c, x in enumerate(add_deposit(acc_ref[...])):
+    for c, x in enumerate(add_parts(acc_ref)):
         sum_ref[c * 256 : (c + 1) * 256, :] = x
     out.send("sums")
+    rates = local_rate(input_blocks(inp), viscosity_blocks(inp, out), magnetic_blocks(inp, out))
+    write_blocks(out.vmem("local"), rates)
+    out.send("local")
 
 
 def arrivals(edge_ref, cnt_ref, me, slab):
@@ -285,10 +306,21 @@
     return live, row, r % 128, velocity
 
 
-def filtered_inner(inp, me):
+def inner_fields(inp):
     recv_ref = inp("inner")
     first = recv_ref[:, 0:TH, :].reshape(NA, 128)
-    second = recv_ref[:, ROW_B : ROW_B + TH, :].reshape(NA, 128)
+    if recv_ref.shape[1] == ROW_EDGE1:
+        return first, recv_ref[:, ROW_B : ROW_B + TH, :].reshape(NA, 128)
+    halves = []
+    for t in range(SECT):
+        x = recv_ref[t, ROW_B : ROW_B + TH // 2, :]
+        halves += [x, pltpu.roll(x, 64, 1)]
+    second = jnp.concatenate(halves, axis=0)
+    return first, jnp.where(lane_iota((NA, 128)) < 64, second, inp("inner_nu")[...].reshape(NA, 128))
+
+
+def filtered_inner(inp, me):
+    first, second = inner_fields(inp)
     lane = lane_iota((1, 128))
     radius = (lane % KR).astype(f32) + 0.5
     left = lane < 64
@@ -311,33 +343,23 @@
     part = jnp.concatenate([part_first, part_second], axis=1)
     low, high = part[: NA // 2], part[NA // 2 :]
     basis_ref, weight_ref, basis_t_ref = inp("basis"), inp("weight"), inp("basis_t")
-    own = pl.ds(pl.multiple_of((me % 4) * TH, TH), TH)
     out = 0.0
     for parity, x in enumerate((low + high, low - high)):
         spectrum = jnp.dot(basis_ref[parity], x, precision=HIGHEST, preferred_element_type=f32)
-        spectrum = spectrum * weight_ref[parity]
-        back = jnp.dot(basis_t_ref[parity, own, :], spectrum, precision=HIGHEST, preferred_element_type=f32)
+        weight = weight_ref[parity]
+        spectrum = spectrum * jnp.concatenate([weight, weight], axis=1)
+        back = jnp.dot(basis_t_ref[parity], spectrum, precision=HIGHEST, preferred_element_type=f32)
         if parity:
             back = jnp.where(me < 4, back, -back)
         out = out + back
     return out[:, :128], out[:, 128:]
 
 
-def fluid_rate(field, nu, magnetic, inp, me, slab):
-    filtered = filtered_inner(inp, me)
-    recv_ref, edge_ref, one_ref, two_ref = inp("inner"), inp("edge"), inp("one"), inp("two")
-    odd = slab % 2 == 1
-    before_sector = (me + SECT - 1) % SECT
-    after_sector = (me + 1) % SECT
-    opposite = (me + SECT // 2) % SECT
+def local_rate(field, nu, magnetic):
     lane = lane_iota((TH, 128))
     row = row_iota((TH, 128))
-    poles = [recv_ref[opposite, 0:TH, :], recv_ref[opposite, ROW_B : ROW_B + TH, :]]
     rates = [[[None, None], [None, None]] for _ in range(3)]
     for z in range(2):
-        ghosts = []
-        for c in range(3):
-            ghosts.append(POLE_SIGNS[c] * lanes(poles[c // 2], -((c % 2) * 64 + z * 32)))
         rolled = [[(pltpu.roll(field[c][z][h], 1, 1), pltpu.roll(field[c][z][h], 127, 1)) for h in range(2)] for c in range(3)]
         for h in range(2):
             radius = lane_iota((1, 128)).astype(f32) + (h * 128 + 0.5)
@@ -348,25 +370,18 @@
             for c in range(3):
                 x = u[c]
                 if h == 0:
-                    prev_r = jnp.where(lane == 0, ghosts[c], rolled[c][0][0])
+                    prev_r = jnp.where(lane == 0, 0.0, rolled[c][0][0])
                     next_r = jnp.where(lane == 127, rolled[c][1][1], rolled[c][0][1])
                 else:
                     prev_r = jnp.where(lane == 0, rolled[c][0][0], rolled[c][1][0])
                     next_r = jnp.where(lane == 127, 0.0, rolled[c][1][1])
-                face = pl.ds((c * 2 + h) * TH, TH)
-                if z == 0:
-                    prev_z = jnp.where(odd, one_ref[face, :], two_ref[face, :])
-                    next_z = field[c][1][h]
-                else:
-                    prev_z = field[c][0][h]
-                    next_z = jnp.where(odd, two_ref[face, :], one_ref[face, :])
-                halo = (c * 2 + z) * 2 + h
-                prev_t = jnp.where(row == 0, edge_ref[before_sector, halo : halo + 1, :], pltpu.roll(x, 1, 0))
-                next_t = jnp.where(row == TH - 1, edge_ref[after_sector, halo : halo + 1, :], pltpu.roll(x, TH - 1, 0))
+                other = field[c][1 - z][h]
+                prev_t = jnp.where(row == 0, 0.0, pltpu.roll(x, 1, 0))
+                next_t = jnp.where(row == TH - 1, 0.0, pltpu.roll(x, TH - 1, 0))
                 lap_rad.append(((radius + 0.5) * (next_r - x) - (radius - 0.5) * (x - prev_r)) * inverse)
-                lap_ax.append(next_z - 2.0 * x + prev_z)
+                lap_ax.append(other - 2.0 * x)
                 grad_rad.append(0.5 * (next_r - prev_r))
-                grad_ax.append(0.5 * (next_z - prev_z))
+                grad_ax.append((0.5 if z == 0 else -0.5) * other)
                 lap_th.append((next_t - 2.0 * x + prev_t) * (1.0 / (radius * radius * (DTHETA * DTHETA))))
                 grad_th.append((next_t - prev_t) * (1.0 / (2.0 * DTHETA * radius)))
             b = [magnetic[c][z][h] for c in range(3)]
@@ -387,8 +402,7 @@
             for c in range(3):
                 azimuth = eddy * lap_th[c] - u[1] * grad_th[c] + coupling[c]
                 if h == 0:
-                    inner = lanes(filtered[c // 2], -((c % 2) * 64 + z * 32))
-                    azimuth = jnp.where(lane < KR, inner, azimuth)
+                    azimuth = jnp.where(lane < KR, 0.0, azimuth)
                 rates[c][z][h] = (
                     eddy * (lap_rad[c] + lap_ax[c])
                     - (u[0] * grad_rad[c] + u[2] * grad_ax[c])
@@ -399,58 +413,119 @@
     return rates
 
 
-def materials(inp, out):
-    nu_s, mag_s = out.vmem("nu"), out.vmem("mag")
+def outer_rate(field, nu, inp, me, slab):
+    filtered = filtered_inner(inp, me)
+    recv_ref, edge_ref, one_ref, two_ref = inp("inner"), inp("edge"), inp("one"), inp("two")
+    before_sector = (me + SECT - 1) % SECT
+    after_sector = (me + 1) % SECT
+    opposite = (me + SECT // 2) % SECT
+    odd = slab % 2 == 1
+    lane = lane_iota((TH, 128))
+    row = row_iota((8, 128))
+    poles = [recv_ref[opposite, 0:TH, :]]
+    if recv_ref.shape[1] == ROW_EDGE1:
+        poles.append(recv_ref[opposite, ROW_B : ROW_B + TH, :])
+    else:
+        pole = recv_ref[opposite, ROW_B : ROW_B + TH // 2, :]
+        poles.append(jnp.concatenate([pole, pltpu.roll(pole, 64, 1)], axis=0))
+    rates = [[[None, None], [None, None]] for _ in range(3)]
+    for z in range(2):
+        for h in range(2):
+            radius = lane_iota((1, 128)).astype(f32) + (h * 128 + 0.5)
+            lap_factor = 1.0 / (radius * radius * (DTHETA * DTHETA))
+            grad_factor = 1.0 / (2.0 * DTHETA * radius)
+            cross = 2.0 * grad_factor / radius
+            eddy, u = nu[z][h], [field[c][z][h] for c in range(3)]
+            by_face = eddy + (0.5 if z == 0 else -0.5) * u[2]
+            end = slab == (0 if z == 0 else lax.axis_size("ax") - 1)
+            halos = []
+            for sector, at, sign in ((before_sector, slice(0, 8), -1.0), (after_sector, slice(TH - 8, TH), 1.0)):
+                f = [edge_ref[sector, (c * 2 + z) * 2 + h : (c * 2 + z) * 2 + h + 1, :] for c in range(3)]
+                nu8, swirl8 = eddy[at], u[1][at]
+                by_halo = nu8 * lap_factor - sign * swirl8 * grad_factor
+                extra = [-sign * cross * nu8 * f[1], sign * cross * nu8 * f[0], 0.0]
+                keep = row == (0 if sign < 0 else 7)
+                if h == 0:
+                    keep = keep & (lane_iota((8, 128)) >= KR)
+                halos.append([jnp.where(keep, by_halo * f[c] + extra[c], 0.0) for c in range(3)])
+            for c in range(3):
+                face = pl.ds((c * 2 + h) * TH, TH)
+                one, two = one_ref[face, :], two_ref[face, :]
+                face = jnp.where(odd, one, two) if z == 0 else jnp.where(odd, two, one)
+                rate = jnp.where(end, 0.0, face) * by_face
+                if h == 0:
+                    offset = (c % 2) * 64 + z * 32
+                    ghost = POLE_SIGNS[c] * lanes(poles[c // 2], -offset)
+                    rate = rate + jnp.where(lane < KR, lanes(filtered[c // 2], -offset), 0.0)
+                    rate = rate + jnp.where(lane == 0, 0.5 * u[0] * ghost, 0.0)
+                rates[c][z][h] = jnp.concatenate(
+                    [rate[:8] + halos[0][c], rate[8 : TH - 8], rate[TH - 8 :] + halos[1][c]], axis=0
+                )
+    return rates
+
+
+def viscosity_blocks(inp, out):
+    nu_s = out.vmem("nu")
     nu_s[...] = inp("nu")[...].astype(f32)
+    return [[nu_s[strided(0, z, h), :] for h in range(2)] for z in range(2)]
+
+
+def magnetic_blocks(inp, out):
+    mag_s = out.vmem("mag")
     mag_s[...] = inp("mag")[...].astype(f32)
-    nu = [[nu_s[strided(0, z, h), :] for h in range(2)] for z in range(2)]
-    magnetic = [[[mag_s[strided(c, z, h), :] for h in range(2)] for z in range(2)] for c in range(3)]
-    return nu, magnetic
+    return [[[mag_s[strided(c, z, h), :] for h in range(2)] for z in range(2)] for c in range(3)]
+
+
+def input_blocks(inp):
+    vel_ref = inp("vel")
+    return [[[vel_ref[strided(c, z, h), :] for h in range(2)] for z in range(2)] for c in range(3)]
+
+
+def blocks(ref):
+    return [[[ref[block(c, z, h), :] for h in range(2)] for z in range(2)] for c in range(3)]
 
 
 def first_kernel(inp, out):
     me = lax.axis_index("az")
     slab = lax.axis_index("ax")
     live, row, col, velocity = arrivals(inp("edge"), inp("cnt"), me, slab)
-    arrived = add_deposit(deposit(row, col, velocity, SECT * CAP))
+    arrived = add_parts(deposit(row, col, velocity, SECT * CAP))
     sum_ref = inp("sums")
     total = [sum_ref[c * 256 : (c + 1) * 256, :] + arrived[c] for c in range(4)]
-    nu, magnetic = materials(inp, out)
-    vel_ref = inp("vel")
-    field = [[[vel_ref[strided(c, z, h), :] for h in range(2)] for z in range(2)] for c in range(3)]
-    rates = fluid_rate(field, nu, magnetic, inp, me, slab)
-    mid_ref, rest_ref, pick_ref = out.vmem("mid"), out.vmem("rest"), out.vmem("pick")
+    nu, field = viscosity_blocks(inp, out), input_blocks(inp)
+    rates = outer_rate(field, nu, inp, me, slab)
+    local_ref = inp("local")
+    mid_ref, rest_ref = out.vmem("mid"), out.vmem("rest")
     mid = [[[None, None], [None, None]] for _ in range(3)]
-    picks = []
-    for c in range(3):
-        halves = []
+    for c in range(3):
         for z in range(2):
             for h in range(2):
                 at = slice((z * 2 + h) * TH, (z * 2 + h + 1) * TH)
                 x, s, n = field[c][z][h], total[c][at], total[3][at]
-                u1 = x + DT * (rates[c][z][h] + 2.0 * (s - n * x))
+                u1 = x + DT * (local_ref[block(c, z, h), :] + rates[c][z][h] + 2.0 * (s - n * x))
                 mid[c][z][h] = u1
                 mid_ref[block(c, z, h), :] = u1
                 rest_ref[block(c, z, h), :] = 0.5 * (x + u1) + DT * (0.8 * s + 0.2 * n * x - n * u1)
-                halves.append(0.08 * x + 0.1 * u1)
-        picks.append(jnp.concatenate(halves, axis=0))
-    write_message(out.vmem("inner"), out.vmem("edge"), mid, [nu[z][0] for z in range(2)], me)
-    send_message(out, out.vmem("edge"))
+    inner_ref = out.vmem("inner")
+    first, second = pack_inner(mid, [nu[z][0] for z in range(2)])
+    inner_ref[0:TH, :] = first
+    inner_ref[TH:, :] = jnp.where(
+        lane_iota((TH // 2, 128)) < 64, second[: TH // 2], pltpu.roll(second[TH // 2 :], 64, 1)
+    )
+    send_inner(out, ROW_EDGE2)
+    write_edges(out.vmem("edge"), mid, me)
+    out.copy(out.vmem("edge"), out.hbm("msg").at[:, ROW_EDGE2:, :])
     write_axial(out.vmem("one"), out.vmem("two"), mid, slab)
     out.send("one")
     out.send("two")
     out.send("mid")
     out.send("rest")
-    for c in range(3):
-        hi, lo = split2(picks[c].T)
-        pick_ref[c * 128 : (c + 1) * 128, 0:256] = hi
-        pick_ref[c * 128 : (c + 1) * 128, 256:512] = lo
-    out.send("pick")
 
 
 def take(pick, row, col, n):
-    rows, cols = one_hot_pair(row, col, n)
-    got = jnp.dot(pick, jnp.concatenate([rows, rows], axis=0), preferred_element_type=f32)
+    got = jnp.dot(pick, one_hot(row, 256, n), preferred_element_type=f32)
+    got = got[:384] + got[384:]
+    cols = row_iota((128, n)) == col
     return [jnp.sum(jnp.where(cols, got[c * 128 : (c + 1) * 128], 0.0), axis=0, keepdims=True) for c in range(3)]
 
 
@@ -459,7 +534,15 @@
     slab = lax.axis_index("ax")
     pc_ref, stay_ref, pv_ref = inp("pc"), inp("stay"), inp("pv")
     kept_ref, arr_ref = out.vmem("kept"), out.vmem("arrived")
-    pick = inp("pick")[...]
+    vel_ref, mid_ref = inp("vel"), inp("mid")
+    parts = []
+    for c in range(3):
+        rows = []
+        for z in range(2):
+            for h in range(2):
+                rows.append(0.08 * vel_ref[strided(c, z, h), :] + 0.1 * mid_ref[block(c, z, h), :])
+        parts.append(split2(jnp.concatenate(rows, axis=0).T))
+    pick = jnp.concatenate([p[0] for p in parts] + [p[1] for p in parts], axis=0)
     for k in range(NP // CHUNK):
         part = pl.ds(k * CHUNK, CHUNK)
         row = local_row(pc_ref[0:1, part], pc_ref[1:2, part], pc_ref[2:3, part], me, slab)
@@ -469,6 +552,13 @@
         for c in range(3):
             kept_ref[c : c + 1, part] = jnp.where(stay, 0.82 * pv_ref[c : c + 1, part] + got[c], 0.0)
     out.send("kept")
+    rates = local_rate(blocks(mid_ref), viscosity_blocks(inp, out), magnetic_blocks(inp, out))
+    rest_ref, part_ref = inp("rest"), out.vmem("part")
+    for c in range(3):
+        for z in range(2):
+            for h in range(2):
+                part_ref[block(c, z, h), :] = rest_ref[block(c, z, h), :] + (0.5 * DT) * rates[c][z][h]
+    out.send("part")
     live, row, col, velocity = arrivals(inp("edge"), inp("cnt"), me, slab)
     got = take(pick, row, col, SECT * CAP)
     for c in range(3):
@@ -476,18 +566,15 @@
     out.send("arrived")
 
 
-def last_kernel(inp, out):
+def second_kernel(inp, out):
     me = lax.axis_index("az")
     slab = lax.axis_index("ax")
-    mid_ref = inp("mid")
-    field = [[[mid_ref[block(c, z, h), :] for h in range(2)] for z in range(2)] for c in range(3)]
-    nu, magnetic = materials(inp, out)
-    rates = fluid_rate(field, nu, magnetic, inp, me, slab)
-    rest_ref, out_ref = inp("rest"), out.vmem("new")
+    rates = outer_rate(blocks(inp("mid")), viscosity_blocks(inp, out), inp, me, slab)
+    part_ref, new_ref = inp("part"), out.vmem("new")
     for c in range(3):
         for z in range(2):
             for h in range(2):
-                out_ref[strided(c, z, h), :] = rest_ref[block(c, z, h), :] + (0.5 * DT) * rates[c][z][h]
+                new_ref[strided(c, z, h), :] = part_ref[block(c, z, h), :] + (0.5 * DT) * rates[c][z][h]
     out.send("new")
 
 
@@ -507,7 +594,12 @@
 
     def in_shape(n):
         shape = ins[n].shape
-        return {"inner": (SECT, ROW_EDGE, 128), "edge": (SECT, shape[1] - ROW_EDGE, 128)}.get(n, shape)
+        if n == "basis_t":
+            return (2, TH, shape[2])
+        if n not in ("inner", "edge", "inner_nu"):
+            return shape
+        part = message_rows(n, shape[1])
+        return (SECT, part.stop - part.start, 128)
 
     hbm = pl.BlockSpec(memory_space=pltpu.HBM)
     return pl.pallas_call(
@@ -536,74 +628,86 @@
     pv, pc = particle_velocity, particle_cell
     tables = {"basis": jnp.asarray(BASIS), "weight": jnp.asarray(MODE_WEIGHT), "basis_t": jnp.asarray(BASIS_T)}
     swap_one = [(i, i ^ 1) for i in range(ax)]
-    swap_two = [(i, ((i + 1) ^ 1) - 1) for i in range(1, ax - 1)]
-
-    def exchange(msg, one, two):
-        one = lax.ppermute(one, "ax", swap_one)
-        two = lax.ppermute(two, "ax", swap_two)
-        return lax.all_to_all(msg, "az", split_axis=0, concat_axis=0, tiled=True), one, two
+    swap_two = []
+    for a in range(SECT):
+        swap_two += [(a * ax + i, a * ax + ((i + 1) ^ 1) - 1) for i in range(1, ax - 1)]
+        swap_two += [(a * ax + i, (a ^ 1) * ax + i) for i in (0, ax - 1)]
+
+    def swap(one, two):
+        return lax.ppermute(one, "ax", swap_one), lax.ppermute(two, ("az", "ax"), swap_two)
+
+    def to_all(msg):
+        return lax.all_to_all(msg, "az", split_axis=0, concat_axis=0, tiled=True)
 
     face = ((384, 128), f32)
     field = ((768, 128), f32)
-    materials_bufs = {"nu": ((256, 128), f32), "mag": field}
-    message_bufs = {"inner": ((ROW_EDGE, 128), f32), "one": face, "two": face}
+    materials = {"nu": ((256, 128), f32), "mag": field}
     msg, one, two, stay = call(
         pack_kernel,
         "pack",
-        {"pc": pc, "pv": pv, "rows": send_rows, "cnt": send_counts, "vel": vel, "nu": nu},
-        {"msg": ((SECT, ROW_EDGE + EDGE1, 128), f32), "one": face, "two": face, "stay": ((1, NP), f32)},
-        message_bufs
-        | {"edge": ((SECT, EDGE1, 128), f32), "stay": ((1, NP), f32), "tmp": ((1024, 128), f32), "nu": ((256, 128), f32)},
+        {"vel": vel, "nu": nu, "pc": pc, "pv": pv, "rows": send_rows, "cnt": send_counts},
+        {"msg": ((SECT, ROW_EDGE1 + EDGE1, 128), f32), "one": face, "two": face, "stay": ((1, NP), f32)},
+        {
+            "inner": ((ROW_EDGE1, 128), f32),
+            "one": face,
+            "two": face,
+            "edge": ((SECT, EDGE1, 128), f32),
+            "stay": ((1, NP), f32),
+            "tmp": ((1024, 128), f32),
+            "nu": ((256, 128), f32),
+        },
         12,
         in_smem=("cnt",),
     )
-    recv, one, two = exchange(msg, one, two)
-    (sums,) = call(
+    one, two = swap(one, two)
+    recv = to_all(msg)
+    sums, local = call(
         scatter_kernel,
         "deposit",
-        {"pc": pc, "stay": stay, "pv": pv},
-        {"sums": ((1024, 128), f32)},
-        {"sums": ((1024, 128), f32), "acc": ((256, 896), f32)},
-        1,
+        {"pc": pc, "stay": stay, "pv": pv, "vel": vel, "nu": nu, "mag": mag},
+        {"sums": ((1024, 128), f32), "local": field},
+        {"sums": ((1024, 128), f32), "acc": ((256, 896), f32), "local": field} | materials,
+        2,
         flops=2 * NP * 256 * 896,
     )
-    msg2, one2, two2, mid, rest, pick = call(
+    msg2, one2, two2, mid, rest = call(
         first_kernel,
         "first_section",
-        {"edge": recv, "cnt": send_counts, "inner": recv, "sums": sums, "nu": nu, "mag": mag, "vel": vel}
+        {"edge": recv, "inner": recv, "cnt": send_counts, "basis": tables["basis"], "sums": sums, "nu": nu, "vel": vel}
         | tables
-        | {"one": one, "two": two},
+        | {"one": one, "two": two, "local": local},
+        {"msg": ((SECT, ROW_EDGE2 + EDGE2, 128), f32), "one": face, "two": face, "mid": field, "rest": field},
         {
-            "msg": ((SECT, ROW_EDGE + EDGE2, 128), f32),
+            "inner": ((ROW_EDGE2, 128), f32),
+            "edge": ((SECT, EDGE2, 128), f32),
             "one": face,
             "two": face,
             "mid": field,
             "rest": field,
-            "pick": ((384, 512), bf16),
+            "nu": ((256, 128), f32),
         },
-        message_bufs
-        | materials_bufs
-        | {"edge": ((SECT, EDGE2, 128), f32), "mid": field, "rest": field, "pick": ((384, 512), bf16)},
-        14,
+        13,
         in_smem=("cnt",),
     )
-    recv2, one2, two2 = exchange(msg2, one2, two2)
-    kept, arrived = call(
+    one2, two2 = swap(one2, two2)
+    recv2 = to_all(msg2)
+    kept, arrived, part = call(
         gather_kernel,
         "take",
-        {"pc": pc, "stay": stay, "pick": pick, "pv": pv, "edge": recv, "cnt": send_counts},
-        {"kept": ((3, NP), f32), "arrived": ((3, 1, SECT * CAP), f32)},
-        {"kept": ((3, NP), f32), "arrived": ((3, 1, SECT * CAP), f32)},
-        2,
+        {"vel": vel, "mid": mid, "pc": pc, "stay": stay, "pv": pv, "nu": nu, "mag": mag, "rest": rest}
+        | {"edge": recv, "cnt": send_counts},
+        {"kept": ((3, NP), f32), "arrived": ((3, 1, SECT * CAP), f32), "part": field},
+        {"kept": ((3, NP), f32), "arrived": ((3, 1, SECT * CAP), f32), "part": field} | materials,
+        3,
         flops=2 * NP * 512 * 384,
         in_smem=("cnt",),
     )
     (new,) = call(
-        last_kernel,
+        second_kernel,
         "second_section",
-        {"mid": mid, "inner": recv2, "nu": nu, "mag": mag} | tables | {"edge": recv2, "one": one2, "two": two2, "rest": rest},
+        {"inner": recv2, "inner_nu": recv} | tables | {"edge": recv2, "mid": mid, "nu": nu, "one": one2, "two": two2, "part": part},
         {"new": field},
-        materials_bufs | {"new": field},
+        {"nu": ((256, 128), f32), "new": field},
         1,
     )
     new = jnp.swapaxes(new.reshape(3, TH, 2, 2, 128), 2, 3).reshape(3, TH, 2, NR)

time: 53.4 us -> 51.8 us (0.970)
  the two profiles are of different devices: /device:TPU:128 before, /device:TPU:233 now
where the time goes in v1:
time: 51.8 us; the launch traced here: 51.5 us
  Pallas kernels  26.2 us (51%)
  starting transfers between devices  14.6 us (28%)
  waiting for transfers between devices  9.86 us (19%)
  between operations  0.84 us (2%)
    pallas_call x5, Pallas kernels, call(): pl.pallas_call(body, out_shape=[jax.ShapeDtypeStruct(*outs[n]) for n in o...  26.2 us
    ppermute x2, waiting for transfers between devices, swap(): lax.ppermute(two, ('az', 'ax'), swap_two)  9.85 us
    all_to_all x2, starting transfers between devices, to_all(): return lax.all_to_all(msg, 'az', split_axis=0, concat_axis=0, tiled=True)  9.84 us
    ppermute x2, starting transfers between devices, swap(): lax.ppermute(two, ('az', 'ax'), swap_two)  3.49 us
    ppermute x2, starting transfers between devices, swap(): lax.ppermute(one, 'ax', swap_one)  1.23 us
  transfers between devices with their start and end apart: 6, of which 2 were waited for; matrix products, arithmetic and copies ran while one was open for 0% of the time, Pallas kernels for 28%

profile of v1, /device:TPU:233, one launch (start us, length us, event | category | flops | bytes accessed | tf_op | source)
XLA Modules:
  0.0 51.5 jit_solution(2553665132949508080)
XLA Ops:
  0.6 2.8 %pack.1 = (f32[8,152,128]{2,1,0:T(8,128)}, f32[384,128]{1,0:T(8,128)}, f32[384,128]{1,0:T(8,128)}, f32[1,8192]{1,0:T(1,128)}) custom-call(f32[768,128]{1,0:T(8,128)} %bitcast.21, bf16[256,128]{1,0:T(8,128)(2,1)} %bitcast.25, s32[3,8192]{1,0:T(4,128)} %refs_2_.8, f32[3,8192]{1,0:T(4,128)} %refs_4_.4, s32[1,8,128]{2,1,0:T(8,128)} %refs_4_.3, s32[8,1,8]{2,1,0:T(1,128)} %refs_9_.1), custom_call_target="tpu_custom_call" | custom-call | bytes 2097152 | tf_op jit(solution)/shard_map/pack/pallas_call | solution.py:605
  3.4 5.3 %all-to-all-start = ((f32[8,152,128]{2,1,0:T(8,128)}), f32[8,152,128]{2,1,0:T(8,128)}, u32[]{:S(2)}, u32[]{:S(2)}) async-start(f32[8,152,128]{2,1,0:T(8,128)} %get-tuple-element.17), calls=%async_computation | async-start | bytes 1245184 | tf_op jit(solution)/shard_map/all_to_all | solution.py:640
  8.7 1.2 %collective-permute-start = (f32[384,128]{1,0:T(8,128)}, f32[384,128]{1,0:T(8,128)}, u32[]{:S(2)}, u32[]{:S(2)}) collective-permute-start(f32[384,128]{1,0:T(8,128)} %get-tuple-element.20), channel_id=1, source_target_pairs={{0,1},{1,0},{2,3},{3,2},{4,5},{5,4},{6,7},{7,6},{8,9},{9,8},{10,11... | collective-permute-start | bytes 589832 | tf_op jit(solution)/shard_map/ppermute | solution.py:637
  9.9 2.3 %collective-permute-start.1 = (f32[384,128]{1,0:T(8,128)}, f32[384,128]{1,0:T(8,128)}, u32[]{:S(2)}, u32[]{:S(2)}) collective-permute-start(f32[384,128]{1,0:T(8,128)} %get-tuple-element.21), channel_id=1, source_target_pairs={{1,2},{2,1},{3,4},{4,3},{5,6},{6,5},{7,8},{8,7},{9,10},{10,9},{11,... | collective-permute-start | bytes 589832 | tf_op jit(solution)/shard_map/ppermute | solution.py:637
  12.3 7.1 %deposit.1 = (f32[1024,128]{1,0:T(8,128)}, f32[768,128]{1,0:T(8,128)}) custom-call(s32[3,8192]{1,0:T(4,128)} %refs_2_.8, f32[1,8192]{1,0:T(1,128)} %get-tuple-element.18.refs_1_.refs_3_, f32[3,8192]{1,0:T(4,128)} %refs_4_.4, f32[768,128]{1,0:T(8,128)} %bitcast.22, bf16[256,128]{1,0:T(8,128)(2,1)} %bitcast.26, bf16[768,128]{1,0:T(8,128)(2,1)} %bitcast.31), custom_call_target="tpu_custom_call" | custom-call | flops 3758096384 | bytes 2097152 | tf_op jit(solution)/shard_map/deposit/pallas_call | solution.py:605
  19.4 0.0 collective-permute-done.refs_9_
  19.4 6.0 %collective-permute-done.1.refs_10_ = f32[384,128]{1,0:T(8,128)} collective-permute-done((f32[384,128]{1,0:T(8,128)}, f32[384,128]{1,0:T(8,128)}, u32[]{:S(2)}, u32[]{:S(2)}) %collective-permute-start.1) | collective-permute-done | bytes 196640 | tf_op jit(solution)/shard_map/ppermute | solution.py:637
  25.4 0.0 all-to-all-done.refs_0_.refs_1_.refs_8_
  25.4 5.0 %first_section.1 = (f32[8,112,128]{2,1,0:T(8,128)}, f32[384,128]{1,0:T(8,128)}, f32[384,128]{1,0:T(8,128)}, f32[768,128]{1,0:T(8,128)}, f32[768,128]{1,0:T(8,128)}) custom-call(f32[8,152,128]{2,1,0:T(8,128)} %all-to-all-done.refs_0_.refs_1_.refs_8_, f32[8,152,128]{2,1,0:T(8,128)} %all-to-all-done.refs_0_.refs_1_.refs_8_, s32[8,1,8]{2,1,0:T(1,128)} %refs_9_.1, ...), custom_call_target="tpu_custom_call" | custom-call | bytes 2097152 | tf_op jit(solution)/shard_map/first_section/pallas_call | solution.py:605
  30.4 4.5 %all-to-all-start.1 = ((f32[8,112,128]{2,1,0:T(8,128)}), f32[8,112,128]{2,1,0:T(8,128)}, u32[]{:S(2)}, u32[]{:S(2)}) async-start(f32[8,112,128]{2,1,0:T(8,128)} %get-tuple-element.23), calls=%async_computation.1 | async-start | bytes 917504 | tf_op jit(solution)/shard_map/all_to_all | solution.py:640
  34.9 0.0 collective-permute-start.2
  34.9 1.1 %collective-permute-start.3 = (f32[384,128]{1,0:T(8,128)}, f32[384,128]{1,0:T(8,128)}, u32[]{:S(2)}, u32[]{:S(2)}) collective-permute-start(f32[384,128]{1,0:T(8,128)} %get-tuple-element.26), channel_id=1, source_target_pairs={{1,2},{2,1},{3,4},{4,3},{5,6},{6,5},{7,8},{8,7},{9,10},{10,9},{11,... | collective-permute-start | bytes 589832 | tf_op jit(solution)/shard_map/ppermute | solution.py:637
  36.1 7.2 %take.1 = (f32[3,8192]{1,0:T(4,128)}, f32[3,1,1024]{2,1,0:T(1,128)}, f32[768,128]{1,0:T(8,128)}) custom-call(f32[768,128]{1,0:T(8,128)} %bitcast.24, f32[768,128]{1,0:T(8,128)} %get-tuple-element.24.refs_1_.refs_6_, s32[3,8192]{1,0:T(4,128)} %refs_2_.8, f32[1,8192]{1,0:T(1,128)} %get-tuple-element.18.refs_1_.refs_3_, f32[3,8192]{1,0:T(4,128)} %refs_4_.4, ...), custom_call_target="tpu_custom_call" | custom-call | flops 3221225472 | bytes 2097152 | tf_op jit(solution)/shard_map/take/pallas_call | solution.py:605
  43.3 0.0 collective-permute-done.2.refs_8_
  43.3 3.9 %collective-permute-done.3.refs_9_ = f32[384,128]{1,0:T(8,128)} collective-permute-done((f32[384,128]{1,0:T(8,128)}, f32[384,128]{1,0:T(8,128)}, u32[]{:S(2)}, u32[]{:S(2)}) %collective-permute-start.3) | collective-permute-done | bytes 196640 | tf_op jit(solution)/shard_map/ppermute | solution.py:637
  47.2 0.0 all-to-all-done.1.refs_0_.refs_5_
  47.2 4.1 %second_section.1 = f32[768,128]{1,0:T(8,128)} custom-call(f32[8,112,128]{2,1,0:T(8,128)} %all-to-all-done.1.refs_0_.refs_5_, f32[8,152,128]{2,1,0:T(8,128)} %all-to-all-done.refs_0_.refs_1_.refs_8_, f32[2,256,256]{2,1,0:T(8,128)} %constant.6.clone.refs_3_.refs_2_, f32[2,256,128]{2,1,0:T(8,128)} %constant.7.clone.refs_7_.refs_3_, ...), custom_call_target="tpu_custom_call" | custom-call | bytes 2097152 | tf_op jit(solution)/shard_map/second_section/pallas_call | solution.py:605
Async XLA Ops:
  3.4 22.0 %all-to-all-start = ((f32[8,152,128]{2,1,0:T(8,128)}), f32[8,152,128]{2,1,0:T(8,128)}, u32[]{:S(2)}, u32[]{:S(2)}) async-start(f32[8,152,128]{2,1,0:T(8,128)} %get-tuple-element.17), calls=%async_computation | async-start | bytes 1245184 | tf_op jit(solution)/shard_map/all_to_all | solution.py:640
  8.7 10.7 %collective-permute-start = (f32[384,128]{1,0:T(8,128)}, f32[384,128]{1,0:T(8,128)}, u32[]{:S(2)}, u32[]{:S(2)}) collective-permute-start(f32[384,128]{1,0:T(8,128)} %get-tuple-element.20), channel_id=1, source_target_pairs={{0,1},{1,0},{2,3},{3,2},{4,5},{5,4},{6,7},{7,6},{8,9},{9,8},{10,11... | collective-permute-start | bytes 589832 | tf_op jit(solution)/shard_map/ppermute | solution.py:637
  9.9 15.5 %collective-permute-start.1 = (f32[384,128]{1,0:T(8,128)}, f32[384,128]{1,0:T(8,128)}, u32[]{:S(2)}, u32[]{:S(2)}) collective-permute-start(f32[384,128]{1,0:T(8,128)} %get-tuple-element.21), channel_id=1, source_target_pairs={{1,2},{2,1},{3,4},{4,3},{5,6},{6,5},{7,8},{8,7},{9,10},{10,9},{11,... | collective-permute-start | bytes 589832 | tf_op jit(solution)/shard_map/ppermute | solution.py:637
  30.4 16.8 %all-to-all-start.1 = ((f32[8,112,128]{2,1,0:T(8,128)}), f32[8,112,128]{2,1,0:T(8,128)}, u32[]{:S(2)}, u32[]{:S(2)}) async-start(f32[8,112,128]{2,1,0:T(8,128)} %get-tuple-element.23), calls=%async_computation.1 | async-start | bytes 917504 | tf_op jit(solution)/shard_map/all_to_all | solution.py:640
  34.9 8.3 %collective-permute-start.2 = (f32[384,128]{1,0:T(8,128)}, f32[384,128]{1,0:T(8,128)}, u32[]{:S(2)}, u32[]{:S(2)}) collective-permute-start(f32[384,128]{1,0:T(8,128)} %get-tuple-element.25), channel_id=1, source_target_pairs={{0,1},{1,0},{2,3},{3,2},{4,5},{5,4},{6,7},{7,6},{8,9},{9,8},{10,11... | collective-permute-start | bytes 589832 | tf_op jit(solution)/shard_map/ppermute | solution.py:637
  34.9 12.2 %collective-permute-start.3 = (f32[384,128]{1,0:T(8,128)}, f32[384,128]{1,0:T(8,128)}, u32[]{:S(2)}, u32[]{:S(2)}) collective-permute-start(f32[384,128]{1,0:T(8,128)} %get-tuple-element.26), channel_id=1, source_target_pairs={{1,2},{2,1},{3,4},{4,3},{5,6},{6,5},{7,8},{8,7},{9,10},{10,9},{11,... | collective-permute-start | bytes 589832 | tf_op jit(solution)/shard_map/ppermute | solution.py:637

commit v2 on v1

--- a/solution.py
+++ b/solution.py
@@ -80,13 +80,6 @@
 def split2(x):
     hi = x.astype(bf16)
     return hi, (x - hi.astype(f32)).astype(bf16)
-
-
-def split3(x):
-    hi = x.astype(bf16)
-    rest = x - hi.astype(f32)
-    mid = rest.astype(bf16)
-    return hi, mid, (rest - mid.astype(f32)).astype(bf16)
 
 
 def pack_inner(field, nu):
@@ -196,36 +189,33 @@
     parts = []
     for k in range(2):
         for c in range(3):
-            parts.append(split3(tmp_ref[pl.ds(k * 512 + c, 64, stride=8), :]))
-    stack = jnp.concatenate([jnp.concatenate([p[s] for p in parts], axis=1) for s in range(3)], axis=0)
+            parts.append(jnp.concatenate(split2(tmp_ref[pl.ds(k * 512 + c, 64, stride=8), :]), axis=1))
     rows_ref, cnt_ref = inp("rows"), inp("cnt")
-    high_iota = row_iota((64, 128))
-    low_iota = row_iota((128, 128))
-    highs, lows, used_lows = [], [], []
     lane = lane_iota((1, 128))
+    listed = [rows_ref[0, t : t + 1, :] for t in range(SECT)]
+    low = jnp.concatenate([one_hot(row % 128, 128, 128) for row in listed], axis=1)
+    high = [row_iota((64, 128)) == row // 128 for row in listed]
+    used_high = []
     for t in range(SECT):
-        row = rows_ref[0, t : t + 1, :]
-        used = (lane < cnt_ref[me, 0, t]).astype(f32)
-        highs.append((high_iota == row // 128).astype(f32).astype(bf16))
-        low = (low_iota == row % 128).astype(f32)
-        lows.append(low)
-        used_lows.append((low * used).astype(bf16))
-    high = jnp.concatenate(highs, axis=1)
+        used = (high[t] & (lane < cnt_ref[me, 0, t])).astype(f32)
+        used_high.append(used.astype(bf16))
+    picked = jnp.dot(
+        jnp.concatenate(parts, axis=0), jnp.concatenate([low, low], axis=0), preferred_element_type=f32
+    )
+    for t in range(SECT):
+        for q in range(6):
+            value = picked[q * 64 : (q + 1) * 64, t * 128 : (t + 1) * 128]
+            edge_ref[t, EDGE_PART + q : EDGE_PART + q + 1, :] = jnp.sum(
+                jnp.where(high[t], value, 0.0), axis=0, keepdims=True
+            )
+    out.copy(edge_ref, out.hbm("msg").at[:, ROW_EDGE1:, :])
     leaving = lax.dot_general(
-        high, jnp.concatenate(used_lows, axis=1), (((1,), (1,)), ((), ())), preferred_element_type=f32
+        jnp.concatenate(used_high, axis=1), low, (((1,), (1,)), ((), ())), preferred_element_type=f32
     )
     stay = 1.0 - leaving
     for i in range(64):
         stay_ref[0:1, i * 128 : (i + 1) * 128] = stay[i : i + 1, :]
     out.send("stay")
-    picked = lax.dot_general(
-        stack, jnp.concatenate([high, high, high], axis=0), (((0,), (0,)), ((), ())), preferred_element_type=f32
-    )
-    for t in range(SECT):
-        for q in range(6):
-            value = picked[q * 128 : (q + 1) * 128, t * 128 : (t + 1) * 128] * lows[t]
-            edge_ref[t, EDGE_PART + q : EDGE_PART + q + 1, :] = jnp.sum(value, axis=0, keepdims=True)
-    out.copy(edge_ref, out.hbm("msg").at[:, ROW_EDGE1:, :])
 
 
 def local_row(theta, r, z, me, slab):
@@ -575,7 +565,8 @@
         for z in range(2):
             for h in range(2):
                 new_ref[strided(c, z, h), :] = part_ref[block(c, z, h), :] + (0.5 * DT) * rates[c][z][h]
-    out.send("new")
+        rows = pl.ds(c * 256, 256)
+        out.copy(new_ref.at[rows, :], out.hbm("new").at[rows, :])
 
 
 def call(kernel, name, ins, outs, bufs, copies, flops=0, in_smem=()):
@@ -631,7 +622,7 @@
     swap_two = []
     for a in range(SECT):
         swap_two += [(a * ax + i, a * ax + ((i + 1) ^ 1) - 1) for i in range(1, ax - 1)]
-        swap_two += [(a * ax + i, (a ^ 1) * ax + i) for i in (0, ax - 1)]
+        swap_two += [(a * ax + i, (a ^ 2) * ax + i) for i in (0, ax - 1)]
 
     def swap(one, two):
         return lax.ppermute(one, "ax", swap_one), lax.ppermute(two, ("az", "ax"), swap_two)
@@ -708,7 +699,7 @@
         {"inner": recv2, "inner_nu": recv} | tables | {"edge": recv2, "mid": mid, "nu": nu, "one": one2, "two": two2, "part": part},
         {"new": field},
         {"nu": ((256, 128), f32), "new": field},
-        1,
+        3,
     )
     new = jnp.swapaxes(new.reshape(3, TH, 2, 2, 128), 2, 3).reshape(3, TH, 2, NR)
     return new, kept, jnp.swapaxes(arrived, 0, 1)

time: 51.8 us -> 50.1 us (0.967)
  the two profiles are of different devices: /device:TPU:233 before, /device:TPU:128 now
where the time goes in v2:
time: 50.1 us; the launch traced here: 49.7 us
  Pallas kernels  25.9 us (52%)
  starting transfers between devices  13.8 us (28%)
  waiting for transfers between devices  9.1 us (18%)
  between operations  0.87 us (2%)
    pallas_call x5, Pallas kernels, call(): pl.pallas_call(body, out_shape=[jax.ShapeDtypeStruct(*outs[n]) for n in o...  25.9 us
    all_to_all x2, starting transfers between devices, to_all(): return lax.all_to_all(msg, 'az', split_axis=0, concat_axis=0, tiled=True)  9.54 us
    all_to_all x2, waiting for transfers between devices, to_all(): return lax.all_to_all(msg, 'az', split_axis=0, concat_axis=0, tiled=True)  8.7 us
    ppermute x2, starting transfers between devices, swap(): lax.ppermute(two, ('az', 'ax'), swap_two)  4.18 us
  transfers between devices with their start and end apart: 6, of which 3 were waited for; matrix products, arithmetic and copies ran while one was open for 0% of the time, Pallas kernels for 29%

profile of v2, /device:TPU:128, one launch (start us, length us, event | category | flops | bytes accessed | tf_op | source)
XLA Modules:
  0.0 49.7 jit_solution(7602125790098262294)
XLA Ops:
  0.6 2.5 %pack.1 = (f32[8,152,128]{2,1,0:T(8,128)}, f32[384,128]{1,0:T(8,128)}, f32[384,128]{1,0:T(8,128)}, f32[1,8192]{1,0:T(1,128)}) custom-call(f32[768,128]{1,0:T(8,128)} %bitcast.21, bf16[256,128]{1,0:T(8,128)(2,1)} %bitcast.25, s32[3,8192]{1,0:T(4,128)} %refs_2_.8, f32[3,8192]{1,0:T(4,128)} %refs_4_.4, s32[1,8,128]{2,1,0:T(8,128)} %refs_4_.3, s32[8,1,8]{2,1,0:T(1,128)} %refs_9_.1), custom_call_target="tpu_custom_call" | custom-call | bytes 2097152 | tf_op jit(solution)/shard_map/pack/pallas_call | solution.py:596
  3.2 5.4 %all-to-all-start = ((f32[8,152,128]{2,1,0:T(8,128)}), f32[8,152,128]{2,1,0:T(8,128)}, u32[]{:S(2)}, u32[]{:S(2)}) async-start(f32[8,152,128]{2,1,0:T(8,128)} %get-tuple-element.17), calls=%async_computation | async-start | bytes 1245184 | tf_op jit(solution)/shard_map/all_to_all | solution.py:631
  8.6 0.0 collective-permute-start
  8.6 2.4 %collective-permute-start.1 = (f32[384,128]{1,0:T(8,128)}, f32[384,128]{1,0:T(8,128)}, u32[]{:S(2)}, u32[]{:S(2)}) collective-permute-start(f32[384,128]{1,0:T(8,128)} %get-tuple-element.21), channel_id=1, source_target_pairs={{1,2},{2,1},{3,4},{4,3},{5,6},{6,5},{7,8},{8,7},{9,10},{10,9},{11,... | collective-permute-start | bytes 589832 | tf_op jit(solution)/shard_map/ppermute | solution.py:628
  11.0 7.1 %deposit.1 = (f32[1024,128]{1,0:T(8,128)}, f32[768,128]{1,0:T(8,128)}) custom-call(s32[3,8192]{1,0:T(4,128)} %refs_2_.8, f32[1,8192]{1,0:T(1,128)} %get-tuple-element.18.refs_1_.refs_3_, f32[3,8192]{1,0:T(4,128)} %refs_4_.4, f32[768,128]{1,0:T(8,128)} %bitcast.22, bf16[256,128]{1,0:T(8,128)(2,1)} %bitcast.26, bf16[768,128]{1,0:T(8,128)(2,1)} %bitcast.31), custom_call_target="tpu_custom_call" | custom-call | flops 3758096384 | bytes 2097152 | tf_op jit(solution)/shard_map/deposit/pallas_call | solution.py:596
  18.1 0.0 collective-permute-done.refs_9_
  18.1 0.0 collective-permute-done.1.refs_10_
  18.1 5.3 %all-to-all-done.refs_0_.refs_1_.refs_8_ = f32[8,152,128]{2,1,0:T(8,128)} async-done(((f32[8,152,128]{2,1,0:T(8,128)}), f32[8,152,128]{2,1,0:T(8,128)}, u32[]{:S(2)}, u32[]{:S(2)}) %all-to-all-start) | async-done | bytes 622624 | tf_op jit(solution)/shard_map/all_to_all | solution.py:631
  23.4 5.0 %first_section.1 = (f32[8,112,128]{2,1,0:T(8,128)}, f32[384,128]{1,0:T(8,128)}, f32[384,128]{1,0:T(8,128)}, f32[768,128]{1,0:T(8,128)}, f32[768,128]{1,0:T(8,128)}) custom-call(f32[8,152,128]{2,1,0:T(8,128)} %all-to-all-done.refs_0_.refs_1_.refs_8_, f32[8,152,128]{2,1,0:T(8,128)} %all-to-all-done.refs_0_.refs_1_.refs_8_, s32[8,1,8]{2,1,0:T(1,128)} %refs_9_.1, ...), custom_call_target="tpu_custom_call" | custom-call | bytes 2097152 | tf_op jit(solution)/shard_map/first_section/pallas_call | solution.py:596
  28.4 4.1 %all-to-all-start.1 = ((f32[8,112,128]{2,1,0:T(8,128)}), f32[8,112,128]{2,1,0:T(8,128)}, u32[]{:S(2)}, u32[]{:S(2)}) async-start(f32[8,112,128]{2,1,0:T(8,128)} %get-tuple-element.23), calls=%async_computation.1 | async-start | bytes 917504 | tf_op jit(solution)/shard_map/all_to_all | solution.py:631
  32.5 0.1 collective-permute-start.2
  32.6 1.8 %collective-permute-start.3 = (f32[384,128]{1,0:T(8,128)}, f32[384,128]{1,0:T(8,128)}, u32[]{:S(2)}, u32[]{:S(2)}) collective-permute-start(f32[384,128]{1,0:T(8,128)} %get-tuple-element.26), channel_id=1, source_target_pairs={{1,2},{2,1},{3,4},{4,3},{5,6},{6,5},{7,8},{8,7},{9,10},{10,9},{11,... | collective-permute-start | bytes 589832 | tf_op jit(solution)/shard_map/ppermute | solution.py:628
  34.4 7.2 %take.1 = (f32[3,8192]{1,0:T(4,128)}, f32[3,1,1024]{2,1,0:T(1,128)}, f32[768,128]{1,0:T(8,128)}) custom-call(f32[768,128]{1,0:T(8,128)} %bitcast.24, f32[768,128]{1,0:T(8,128)} %get-tuple-element.24.refs_1_.refs_6_, s32[3,8192]{1,0:T(4,128)} %refs_2_.8, f32[1,8192]{1,0:T(1,128)} %get-tuple-element.18.refs_1_.refs_3_, f32[3,8192]{1,0:T(4,128)} %refs_4_.4, ...), custom_call_target="tpu_custom_call" | custom-call | flops 3221225472 | bytes 2097152 | tf_op jit(solution)/shard_map/take/pallas_call | solution.py:596
  41.6 0.0 collective-permute-done.2.refs_8_
  41.6 0.4 collective-permute-done.3.refs_9_
  42.0 3.4 %all-to-all-done.1.refs_0_.refs_5_ = f32[8,112,128]{2,1,0:T(8,128)} async-done(((f32[8,112,128]{2,1,0:T(8,128)}), f32[8,112,128]{2,1,0:T(8,128)}, u32[]{:S(2)}, u32[]{:S(2)}) %all-to-all-start.1) | async-done | bytes 458784 | tf_op jit(solution)/shard_map/all_to_all | solution.py:631
  45.5 4.1 %second_section.1 = f32[768,128]{1,0:T(8,128)} custom-call(f32[8,112,128]{2,1,0:T(8,128)} %all-to-all-done.1.refs_0_.refs_5_, f32[8,152,128]{2,1,0:T(8,128)} %all-to-all-done.refs_0_.refs_1_.refs_8_, f32[2,256,256]{2,1,0:T(8,128)} %constant.6.clone.refs_3_.refs_2_, f32[2,256,128]{2,1,0:T(8,128)} %constant.7.clone.refs_7_.refs_3_, ...), custom_call_target="tpu_custom_call" | custom-call | bytes 2097152 | tf_op jit(solution)/shard_map/second_section/pallas_call | solution.py:596
Async XLA Ops:
  3.2 20.2 %all-to-all-start = ((f32[8,152,128]{2,1,0:T(8,128)}), f32[8,152,128]{2,1,0:T(8,128)}, u32[]{:S(2)}, u32[]{:S(2)}) async-start(f32[8,152,128]{2,1,0:T(8,128)} %get-tuple-element.17), calls=%async_computation | async-start | bytes 1245184 | tf_op jit(solution)/shard_map/all_to_all | solution.py:631
  8.6 9.5 %collective-permute-start = (f32[384,128]{1,0:T(8,128)}, f32[384,128]{1,0:T(8,128)}, u32[]{:S(2)}, u32[]{:S(2)}) collective-permute-start(f32[384,128]{1,0:T(8,128)} %get-tuple-element.20), channel_id=1, source_target_pairs={{0,1},{1,0},{2,3},{3,2},{4,5},{5,4},{6,7},{7,6},{8,9},{9,8},{10,11... | collective-permute-start | bytes 589832 | tf_op jit(solution)/shard_map/ppermute | solution.py:628
  8.6 9.5 %collective-permute-start.1 = (f32[384,128]{1,0:T(8,128)}, f32[384,128]{1,0:T(8,128)}, u32[]{:S(2)}, u32[]{:S(2)}) collective-permute-start(f32[384,128]{1,0:T(8,128)} %get-tuple-element.21), channel_id=1, source_target_pairs={{1,2},{2,1},{3,4},{4,3},{5,6},{6,5},{7,8},{8,7},{9,10},{10,9},{11,... | collective-permute-start | bytes 589832 | tf_op jit(solution)/shard_map/ppermute | solution.py:628
  28.4 17.1 %all-to-all-start.1 = ((f32[8,112,128]{2,1,0:T(8,128)}), f32[8,112,128]{2,1,0:T(8,128)}, u32[]{:S(2)}, u32[]{:S(2)}) async-start(f32[8,112,128]{2,1,0:T(8,128)} %get-tuple-element.23), calls=%async_computation.1 | async-start | bytes 917504 | tf_op jit(solution)/shard_map/all_to_all | solution.py:631
  32.5 9.1 %collective-permute-start.2 = (f32[384,128]{1,0:T(8,128)}, f32[384,128]{1,0:T(8,128)}, u32[]{:S(2)}, u32[]{:S(2)}) collective-permute-start(f32[384,128]{1,0:T(8,128)} %get-tuple-element.25), channel_id=1, source_target_pairs={{0,1},{1,0},{2,3},{3,2},{4,5},{5,4},{6,7},{7,6},{8,9},{9,8},{10,11... | collective-permute-start | bytes 589832 | tf_op jit(solution)/shard_map/ppermute | solution.py:628
  32.6 9.4 %collective-permute-start.3 = (f32[384,128]{1,0:T(8,128)}, f32[384,128]{1,0:T(8,128)}, u32[]{:S(2)}, u32[]{:S(2)}) collective-permute-start(f32[384,128]{1,0:T(8,128)} %get-tuple-element.26), channel_id=1, source_target_pairs={{1,2},{2,1},{3,4},{4,3},{5,6},{6,5},{7,8},{8,7},{9,10},{10,9},{11,... | collective-permute-start | bytes 589832 | tf_op jit(solution)/shard_map/ppermute | solution.py:628

commit v3 on v2

--- a/solution.py
+++ b/solution.py
@@ -25,8 +25,8 @@
 VMEM_LIMIT = 65408 * 1024
 
 ROW_B = 64
-ROW_EDGE1 = 128
-ROW_EDGE2 = 96
+ROW_EDGE = 96
+EDGE_BOUND = 12
 EDGE_PART = 16
 EDGE1 = 24
 EDGE2 = 16
@@ -95,15 +95,56 @@
     return first, second
 
 
-def write_edges(edge_ref, field, me):
-    up = (me + 1) % SECT
+def azimuth_factors():
+    lane = lane_iota((1, 128))
+    radius = (lane % KR).astype(f32) + 0.5
+    lap = 1.0 / (radius * radius * (DTHETA * DTHETA))
+    grad = 1.0 / (2.0 * DTHETA * radius)
+    return lane < 64, lap, grad, jnp.where(lane < 64, -2.0, 2.0) / radius
+
+
+def both_halves(x, left):
+    side = lane_iota((1, 128)) < 64
+    return jnp.where(side == left, x, pltpu.roll(x, 64, 1))
+
+
+def azimuth_inner(first, second):
+    left, lap_factor, grad_factor, cross = azimuth_factors()
+    row = row_iota((TH, 128))
+    nu, swirl = both_halves(second, False), both_halves(first, False)
+
+    def differences(x):
+        after = jnp.where(row == TH - 1, 0.0, pltpu.roll(x, TH - 1, 0))
+        before = jnp.where(row == 0, 0.0, pltpu.roll(x, 1, 0))
+        return (after - 2.0 * x + before) * lap_factor, (after - before) * grad_factor
+
+    lap, grad = differences(first)
+    part_first = nu * lap - swirl * grad + cross * nu * pltpu.roll(grad, 64, 1)
+    lap, grad = differences(second)
+    return part_first, jnp.where(left, nu * lap - swirl * grad, 0.0)
+
+
+def write_message(inner_ref, edge_ref, field, nu, me):
+    first, second = pack_inner(field, nu)
+    part_first, part_second = azimuth_inner(first, second)
+    inner_ref[0:TH, :] = part_first
+    inner_ref[TH:, :] = part_second[: TH // 2] + pltpu.roll(part_second[TH // 2 :], 64, 1)
+    turned = jnp.concatenate([first, second], axis=0).T
+    up, opposite = (me + 1) % SECT, (me + SECT // 2) % SECT
+    bounds = [first[0:1], second[0:1], first[TH - 1 : TH], second[TH - 1 : TH]]
+    for t in range(SECT):
+        for k in range(4):
+            edge_ref[t, EDGE_BOUND + k : EDGE_BOUND + k + 1, :] = bounds[k]
     for c in range(3):
         for z in range(2):
             for h in range(2):
                 x = field[c][z][h]
                 row = (c * 2 + z) * 2 + h
                 for t in range(SECT):
-                    edge_ref[t, row : row + 1, :] = jnp.where(t == up, x[TH - 1 : TH], x[0:1])
+                    edge = jnp.where(t == up, x[TH - 1 : TH], x[0:1])
+                    if row < 4:
+                        edge = jnp.where(t == opposite, turned[row * 32 : row * 32 + 1], edge)
+                    edge_ref[t, row : row + 1, :] = edge
 
 
 def send_inner(out, rows):
@@ -121,18 +162,15 @@
             two_ref[rows, :] = jnp.where(odd, high, low)
 
 
-def message_rows(name, rows):
-    edge = ROW_EDGE1 if rows == ROW_EDGE1 + EDGE1 else ROW_EDGE2
-    return {"inner": slice(0, edge), "edge": slice(edge, rows), "inner_nu": slice(ROW_B, edge)}[name]
-
-
 class Inputs:
     def __init__(self, names, refs, bufs, sems):
         self.refs = dict(zip(names, bufs))
         self.copies = {}
         for i, (name, ref, buf) in enumerate(zip(names, refs, bufs)):
-            if name in ("inner", "edge", "inner_nu"):
-                ref = ref.at[:, message_rows(name, ref.shape[1]), :]
+            if name == "inner":
+                ref = ref.at[:, 0:ROW_EDGE, :]
+            if name == "edge":
+                ref = ref.at[:, ROW_EDGE:, :]
             if name == "basis_t":
                 own = lax.axis_index("az") % 4
                 ref = ref.at[:, pl.ds(pl.multiple_of(own * TH, TH), TH), :]
@@ -175,13 +213,11 @@
     field = [[[vel_ref[strided(c, z, h), :] for h in range(2)] for z in range(2)] for c in range(3)]
     nu_s[...] = nu_ref[...].astype(f32)
     nu = [nu_s[pl.ds(z, TH, stride=4), :] for z in range(2)]
-    inner_ref = out.vmem("inner")
-    inner_ref[0:TH, :], inner_ref[TH:, :] = pack_inner(field, nu)
-    send_inner(out, ROW_EDGE1)
+    write_message(out.vmem("inner"), edge_ref, field, nu, me)
+    send_inner(out, ROW_EDGE)
     write_axial(out.vmem("one"), out.vmem("two"), field, lax.axis_index("ax"))
     out.send("one")
     out.send("two")
-    write_edges(edge_ref, field, me)
     pv_ref, pc_ref = inp("pv"), inp("pc")
     for i in range(64):
         tmp_ref[i * 8 : i * 8 + 3, :] = pv_ref[:, i * 128 : (i + 1) * 128]
@@ -208,7 +244,7 @@
             edge_ref[t, EDGE_PART + q : EDGE_PART + q + 1, :] = jnp.sum(
                 jnp.where(high[t], value, 0.0), axis=0, keepdims=True
             )
-    out.copy(edge_ref, out.hbm("msg").at[:, ROW_EDGE1:, :])
+    out.copy(edge_ref, out.hbm("msg").at[:, ROW_EDGE:, :])
     leaving = lax.dot_general(
         jnp.concatenate(used_high, axis=1), low, (((1,), (1,)), ((), ())), preferred_element_type=f32
     )
@@ -296,41 +332,37 @@
     return live, row, r % 128, velocity
 
 
-def inner_fields(inp):
-    recv_ref = inp("inner")
-    first = recv_ref[:, 0:TH, :].reshape(NA, 128)
-    if recv_ref.shape[1] == ROW_EDGE1:
-        return first, recv_ref[:, ROW_B : ROW_B + TH, :].reshape(NA, 128)
-    halves = []
+def whole_azimuth_part(inp):
+    recv_ref, edge_ref = inp("inner"), inp("edge")
+    left, lap_factor, grad_factor, cross = azimuth_factors()
+    bounds = []
+    for k in range(4):
+        at = EDGE_BOUND + k
+        bounds.append(jnp.concatenate([edge_ref[t, at : at + 1, :] for t in range(SECT)], axis=0))
+
+    def share(near, far, sign):
+        nu, swirl = both_halves(near[1], False), both_halves(near[0], False)
+        factor = nu * lap_factor - sign * swirl * grad_factor
+        turn = cross * nu * pltpu.roll(sign * far[0] * grad_factor, 64, 1)
+        return factor * far[0] + turn, jnp.where(left, factor * far[1], 0.0)
+
+    begin, end = bounds[:2], bounds[2:]
+    at_begin = share(begin, [pltpu.roll(x, 1, 0) for x in end], -1.0)
+    at_end = share(end, [pltpu.roll(x, SECT - 1, 0) for x in begin], 1.0)
+    row = row_iota((8, 128))
+    out = ([], [])
     for t in range(SECT):
-        x = recv_ref[t, ROW_B : ROW_B + TH // 2, :]
-        halves += [x, pltpu.roll(x, 64, 1)]
-    second = jnp.concatenate(halves, axis=0)
-    return first, jnp.where(lane_iota((NA, 128)) < 64, second, inp("inner_nu")[...].reshape(NA, 128))
+        folded = recv_ref[t, ROW_B : ROW_B + TH // 2, :]
+        second = jnp.concatenate([folded, pltpu.roll(folded, 64, 1)], axis=0)
+        for k, x in enumerate((recv_ref[t, 0:TH, :], jnp.where(left, second, 0.0))):
+            out[k].append(x[:8] + jnp.where(row == 0, at_begin[k][t : t + 1], 0.0))
+            out[k].append(x[8 : TH - 8])
+            out[k].append(x[TH - 8 :] + jnp.where(row == 7, at_end[k][t : t + 1], 0.0))
+    return jnp.concatenate(out[0], axis=0), jnp.concatenate(out[1], axis=0)
 
 
 def filtered_inner(inp, me):
-    first, second = inner_fields(inp)
-    lane = lane_iota((1, 128))
-    radius = (lane % KR).astype(f32) + 0.5
-    left = lane < 64
-    first_swap = pltpu.roll(first, 64, 1)
-    second_swap = pltpu.roll(second, 64, 1)
-    nu = jnp.where(left, second_swap, second)
-    swirl = jnp.where(left, first_swap, first)
-
-    def differences(x):
-        after = pltpu.roll(x, NA - 1, 0)
-        before = pltpu.roll(x, 1, 0)
-        lap = (after - 2.0 * x + before) * (1.0 / (radius * radius * (DTHETA * DTHETA)))
-        return lap, (after - before) * (1.0 / (2.0 * DTHETA * radius))
-
-    lap, grad = differences(first)
-    cross = jnp.where(left, -2.0, 2.0) / radius
-    part_first = nu * lap - swirl * grad + cross * nu * pltpu.roll(grad, 64, 1)
-    lap, grad = differences(second)
-    part_second = jnp.where(left, nu * lap - swirl * grad, 0.0)
-    part = jnp.concatenate([part_first, part_second], axis=1)
+    part = jnp.concatenate(whole_azimuth_part(inp), axis=1)
     low, high = part[: NA // 2], part[NA // 2 :]
     basis_ref, weight_ref, basis_t_ref = inp("basis"), inp("weight"), inp("basis_t")
     out = 0.0
@@ -405,19 +437,14 @@
 
 def outer_rate(field, nu, inp, me, slab):
     filtered = filtered_inner(inp, me)
-    recv_ref, edge_ref, one_ref, two_ref = inp("inner"), inp("edge"), inp("one"), inp("two")
+    edge_ref, one_ref, two_ref = inp("edge"), inp("one"), inp("two")
     before_sector = (me + SECT - 1) % SECT
     after_sector = (me + 1) % SECT
     opposite = (me + SECT // 2) % SECT
     odd = slab % 2 == 1
     lane = lane_iota((TH, 128))
     row = row_iota((8, 128))
-    poles = [recv_ref[opposite, 0:TH, :]]
-    if recv_ref.shape[1] == ROW_EDGE1:
-        poles.append(recv_ref[opposite, ROW_B : ROW_B + TH, :])
-    else:
-        pole = recv_ref[opposite, ROW_B : ROW_B + TH // 2, :]
-        poles.append(jnp.concatenate([pole, pltpu.roll(pole, 64, 1)], axis=0))
+    turned = jnp.concatenate([edge_ref[opposite, 0:8, :], jnp.zeros((120, 128), f32)], axis=0).T
     rates = [[[None, None], [None, None]] for _ in range(3)]
     for z in range(2):
         for h in range(2):
@@ -445,7 +472,8 @@
                 rate = jnp.where(end, 0.0, face) * by_face
                 if h == 0:
                     offset = (c % 2) * 64 + z * 32
-                    ghost = POLE_SIGNS[c] * lanes(poles[c // 2], -offset)
+                    pole = turned[TH:] if c == 2 else turned[:TH]
+                    ghost = POLE_SIGNS[c] * lanes(pole, -((c % 2) * 2 + z))
                     rate = rate + jnp.where(lane < KR, lanes(filtered[c // 2], -offset), 0.0)
                     rate = rate + jnp.where(lane == 0, 0.5 * u[0] * ghost, 0.0)
                 rates[c][z][h] = jnp.concatenate(
@@ -496,15 +524,9 @@
                 mid[c][z][h] = u1
                 mid_ref[block(c, z, h), :] = u1
                 rest_ref[block(c, z, h), :] = 0.5 * (x + u1) + DT * (0.8 * s + 0.2 * n * x - n * u1)
-    inner_ref = out.vmem("inner")
-    first, second = pack_inner(mid, [nu[z][0] for z in range(2)])
-    inner_ref[0:TH, :] = first
-    inner_ref[TH:, :] = jnp.where(
-        lane_iota((TH // 2, 128)) < 64, second[: TH // 2], pltpu.roll(second[TH // 2 :], 64, 1)
-    )
-    send_inner(out, ROW_EDGE2)
-    write_edges(out.vmem("edge"), mid, me)
-    out.copy(out.vmem("edge"), out.hbm("msg").at[:, ROW_EDGE2:, :])
+    write_message(out.vmem("inner"), out.vmem("edge"), mid, [nu[z][0] for z in range(2)], me)
+    send_inner(out, ROW_EDGE)
+    out.copy(out.vmem("edge"), out.hbm("msg").at[:, ROW_EDGE:, :])
     write_axial(out.vmem("one"), out.vmem("two"), mid, slab)
     out.send("one")
     out.send("two")
@@ -587,10 +609,7 @@
         shape = ins[n].shape
         if n == "basis_t":
             return (2, TH, shape[2])
-        if n not in ("inner", "edge", "inner_nu"):
-            return shape
-        part = message_rows(n, shape[1])
-        return (SECT, part.stop - part.start, 128)
+        return {"inner": (SECT, ROW_EDGE, 128), "edge": (SECT, shape[1] - ROW_EDGE, 128)}.get(n, shape)
 
     hbm = pl.BlockSpec(memory_space=pltpu.HBM)
     return pl.pallas_call(
@@ -637,9 +656,9 @@
         pack_kernel,
         "pack",
         {"vel": vel, "nu": nu, "pc": pc, "pv": pv, "rows": send_rows, "cnt": send_counts},
-        {"msg": ((SECT, ROW_EDGE1 + EDGE1, 128), f32), "one": face, "two": face, "stay": ((1, NP), f32)},
+        {"msg": ((SECT, ROW_EDGE + EDGE1, 128), f32), "one": face, "two": face, "stay": ((1, NP), f32)},
         {
-            "inner": ((ROW_EDGE1, 128), f32),
+            "inner": ((ROW_EDGE, 128), f32),
             "one": face,
             "two": face,
             "edge": ((SECT, EDGE1, 128), f32),
@@ -667,9 +686,9 @@
         {"edge": recv, "inner": recv, "cnt": send_counts, "basis": tables["basis"], "sums": sums, "nu": nu, "vel": vel}
         | tables
         | {"one": one, "two": two, "local": local},
-        {"msg": ((SECT, ROW_EDGE2 + EDGE2, 128), f32), "one": face, "two": face, "mid": field, "rest": field},
+        {"msg": ((SECT, ROW_EDGE + EDGE2, 128), f32), "one": face, "two": face, "mid": field, "rest": field},
         {
-            "inner": ((ROW_EDGE2, 128), f32),
+            "inner": ((ROW_EDGE, 128), f32),
             "edge": ((SECT, EDGE2, 128), f32),
             "one": face,
             "two": face,
@@ -696,7 +715,7 @@
     (new,) = call(
         second_kernel,
         "second_section",
-        {"inner": recv2, "inner_nu": recv} | tables | {"edge": recv2, "mid": mid, "nu": nu, "one": one2, "two": two2, "part": part},
+        {"inner": recv2} | tables | {"edge": recv2, "mid": mid, "nu": nu, "one": one2, "two": two2, "part": part},
         {"new": field},
         {"nu": ((256, 128), f32), "new": field},
         3,

time: 50.1 us -> 48.4 us (0.966)
  waiting for transfers between devices: 9.1 us -> 7.7 us
    all_to_all x2, waiting for transfers between devices: 8.7 us -> 7.28 us  [to_all(): return lax.all_to_all(msg, 'az', split_axis=0, concat_axis=0, tiled=True)]
  transfers between devices with their start and end apart: 6 -> 6, of which waited for: 3 -> 3; matrix products, arithmetic and copies ran while one was open for 0% -> 0% of each run, Pallas kernels for 29% -> 30%
where the time goes in v3:
time: 48.4 us; the launch traced here: 48 us
  Pallas kernels  25.6 us (53%)
  starting transfers between devices  13.8 us (29%)
  waiting for transfers between devices  7.7 us (16%)
  between operations  0.87 us (2%)
    pallas_call x5, Pallas kernels, call(): pl.pallas_call(body, out_shape=[jax.ShapeDtypeStruct(*outs[n]) for n in o...  25.6 us
    all_to_all x2, starting transfers between devices, to_all(): return lax.all_to_all(msg, 'az', split_axis=0, concat_axis=0, tiled=True)  9.54 us
    all_to_all x2, waiting for transfers between devices, to_all(): return lax.all_to_all(msg, 'az', split_axis=0, concat_axis=0, tiled=True)  7.28 us
    ppermute x2, starting transfers between devices, swap(): lax.ppermute(two, ('az', 'ax'), swap_two)  4.16 us
  transfers between devices with their start and end apart: 6, of which 3 were waited for; matrix products, arithmetic and copies ran while one was open for 0% of the time, Pallas kernels for 30%

profile of v3, /device:TPU:128, one launch (start us, length us, event | category | flops | bytes accessed | tf_op | source)
XLA Modules:
  0.0 48.0 jit_solution(10974733032127470957)
XLA Ops:
  0.6 2.7 %pack.1 = (f32[8,120,128]{2,1,0:T(8,128)}, f32[384,128]{1,0:T(8,128)}, f32[384,128]{1,0:T(8,128)}, f32[1,8192]{1,0:T(1,128)}) custom-call(f32[768,128]{1,0:T(8,128)} %bitcast.21, bf16[256,128]{1,0:T(8,128)(2,1)} %bitcast.25, s32[3,8192]{1,0:T(4,128)} %refs_2_.8, f32[3,8192]{1,0:T(4,128)} %refs_4_.3, s32[1,8,128]{2,1,0:T(8,128)} %refs_4_.2, s32[8,1,8]{2,1,0:T(1,128)} %refs_9_.1), custom_call_target="tpu_custom_call" | custom-call | bytes 2097152 | tf_op jit(solution)/shard_map/pack/pallas_call | solution.py:615
  3.3 5.4 %all-to-all-start = ((f32[8,120,128]{2,1,0:T(8,128)}), f32[8,120,128]{2,1,0:T(8,128)}, u32[]{:S(2)}, u32[]{:S(2)}) async-start(f32[8,120,128]{2,1,0:T(8,128)} %get-tuple-element.17), calls=%async_computation | async-start | bytes 983040 | tf_op jit(solution)/shard_map/all_to_all | solution.py:650
  8.7 0.0 collective-permute-start
  8.8 2.4 %collective-permute-start.1 = (f32[384,128]{1,0:T(8,128)}, f32[384,128]{1,0:T(8,128)}, u32[]{:S(2)}, u32[]{:S(2)}) collective-permute-start(f32[384,128]{1,0:T(8,128)} %get-tuple-element.21), channel_id=1, source_target_pairs={{1,2},{2,1},{3,4},{4,3},{5,6},{6,5},{7,8},{8,7},{9,10},{10,9},{11,... | collective-permute-start | bytes 589832 | tf_op jit(solution)/shard_map/ppermute | solution.py:647
  11.1 7.1 %deposit.1 = (f32[1024,128]{1,0:T(8,128)}, f32[768,128]{1,0:T(8,128)}) custom-call(s32[3,8192]{1,0:T(4,128)} %refs_2_.8, f32[1,8192]{1,0:T(1,128)} %get-tuple-element.18.refs_1_.refs_3_, f32[3,8192]{1,0:T(4,128)} %refs_4_.3, f32[768,128]{1,0:T(8,128)} %bitcast.22, bf16[256,128]{1,0:T(8,128)(2,1)} %bitcast.26, bf16[768,128]{1,0:T(8,128)(2,1)} %bitcast.31), custom_call_target="tpu_custom_call" | custom-call | flops 3758096384 | bytes 2097152 | tf_op jit(solution)/shard_map/deposit/pallas_call | solution.py:615
  18.3 0.0 collective-permute-done.refs_9_
  18.3 0.0 collective-permute-done.1.refs_10_
  18.3 3.9 %all-to-all-done.refs_0_.refs_1_.refs_8_ = f32[8,120,128]{2,1,0:T(8,128)} async-done(((f32[8,120,128]{2,1,0:T(8,128)}), f32[8,120,128]{2,1,0:T(8,128)}, u32[]{:S(2)}, u32[]{:S(2)}) %all-to-all-start) | async-done | bytes 491552 | tf_op jit(solution)/shard_map/all_to_all | solution.py:650
  22.2 4.9 %first_section.1 = (f32[8,112,128]{2,1,0:T(8,128)}, f32[384,128]{1,0:T(8,128)}, f32[384,128]{1,0:T(8,128)}, f32[768,128]{1,0:T(8,128)}, f32[768,128]{1,0:T(8,128)}) custom-call(f32[8,120,128]{2,1,0:T(8,128)} %all-to-all-done.refs_0_.refs_1_.refs_8_, f32[8,120,128]{2,1,0:T(8,128)} %all-to-all-done.refs_0_.refs_1_.refs_8_, s32[8,1,8]{2,1,0:T(1,128)} %refs_9_.1, ...), custom_call_target="tpu_custom_call" | custom-call | bytes 2097152 | tf_op jit(solution)/shard_map/first_section/pallas_call | solution.py:615
  27.1 4.1 %all-to-all-start.1 = ((f32[8,112,128]{2,1,0:T(8,128)}), f32[8,112,128]{2,1,0:T(8,128)}, u32[]{:S(2)}, u32[]{:S(2)}) async-start(f32[8,112,128]{2,1,0:T(8,128)} %get-tuple-element.23), calls=%async_computation.1 | async-start | bytes 917504 | tf_op jit(solution)/shard_map/all_to_all | solution.py:650
  31.2 0.1 collective-permute-start.2
  31.3 1.8 %collective-permute-start.3 = (f32[384,128]{1,0:T(8,128)}, f32[384,128]{1,0:T(8,128)}, u32[]{:S(2)}, u32[]{:S(2)}) collective-permute-start(f32[384,128]{1,0:T(8,128)} %get-tuple-element.26), channel_id=1, source_target_pairs={{1,2},{2,1},{3,4},{4,3},{5,6},{6,5},{7,8},{8,7},{9,10},{10,9},{11,... | collective-permute-start | bytes 589832 | tf_op jit(solution)/shard_map/ppermute | solution.py:647
  33.1 7.2 %take.1 = (f32[3,8192]{1,0:T(4,128)}, f32[3,1,1024]{2,1,0:T(1,128)}, f32[768,128]{1,0:T(8,128)}) custom-call(f32[768,128]{1,0:T(8,128)} %bitcast.24, f32[768,128]{1,0:T(8,128)} %get-tuple-element.24.refs_1_.refs_5_, s32[3,8192]{1,0:T(4,128)} %refs_2_.8, f32[1,8192]{1,0:T(1,128)} %get-tuple-element.18.refs_1_.refs_3_, f32[3,8192]{1,0:T(4,128)} %refs_4_.3, ...), custom_call_target="tpu_custom_call" | custom-call | flops 3221225472 | bytes 2097152 | tf_op jit(solution)/shard_map/take/pallas_call | solution.py:615
  40.3 0.0 collective-permute-done.2.refs_7_
  40.3 0.4 collective-permute-done.3.refs_8_
  40.7 3.4 %all-to-all-done.1.refs_0_.refs_4_ = f32[8,112,128]{2,1,0:T(8,128)} async-done(((f32[8,112,128]{2,1,0:T(8,128)}), f32[8,112,128]{2,1,0:T(8,128)}, u32[]{:S(2)}, u32[]{:S(2)}) %all-to-all-start.1) | async-done | bytes 458784 | tf_op jit(solution)/shard_map/all_to_all | solution.py:650
  44.1 3.7 %second_section.1 = f32[768,128]{1,0:T(8,128)} custom-call(f32[8,112,128]{2,1,0:T(8,128)} %all-to-all-done.1.refs_0_.refs_4_, f32[2,256,256]{2,1,0:T(8,128)} %constant.6.clone.refs_3_.refs_1_, f32[2,256,128]{2,1,0:T(8,128)} %constant.7.clone.refs_7_.refs_2_, f32[2,256,256]{2,1,0:T(8,128)} %constant.8.clone.refs_8_.refs_3_, ...), custom_call_target="tpu_custom_call" | custom-call | bytes 2097152 | tf_op jit(solution)/shard_map/second_section/pallas_call | solution.py:615
Async XLA Ops:
  3.3 18.8 %all-to-all-start = ((f32[8,120,128]{2,1,0:T(8,128)}), f32[8,120,128]{2,1,0:T(8,128)}, u32[]{:S(2)}, u32[]{:S(2)}) async-start(f32[8,120,128]{2,1,0:T(8,128)} %get-tuple-element.17), calls=%async_computation | async-start | bytes 983040 | tf_op jit(solution)/shard_map/all_to_all | solution.py:650
  8.7 9.5 %collective-permute-start = (f32[384,128]{1,0:T(8,128)}, f32[384,128]{1,0:T(8,128)}, u32[]{:S(2)}, u32[]{:S(2)}) collective-permute-start(f32[384,128]{1,0:T(8,128)} %get-tuple-element.20), channel_id=1, source_target_pairs={{0,1},{1,0},{2,3},{3,2},{4,5},{5,4},{6,7},{7,6},{8,9},{9,8},{10,11... | collective-permute-start | bytes 589832 | tf_op jit(solution)/shard_map/ppermute | solution.py:647
  8.8 9.5 %collective-permute-start.1 = (f32[384,128]{1,0:T(8,128)}, f32[384,128]{1,0:T(8,128)}, u32[]{:S(2)}, u32[]{:S(2)}) collective-permute-start(f32[384,128]{1,0:T(8,128)} %get-tuple-element.21), channel_id=1, source_target_pairs={{1,2},{2,1},{3,4},{4,3},{5,6},{6,5},{7,8},{8,7},{9,10},{10,9},{11,... | collective-permute-start | bytes 589832 | tf_op jit(solution)/shard_map/ppermute | solution.py:647
  27.1 17.1 %all-to-all-start.1 = ((f32[8,112,128]{2,1,0:T(8,128)}), f32[8,112,128]{2,1,0:T(8,128)}, u32[]{:S(2)}, u32[]{:S(2)}) async-start(f32[8,112,128]{2,1,0:T(8,128)} %get-tuple-element.23), calls=%async_computation.1 | async-start | bytes 917504 | tf_op jit(solution)/shard_map/all_to_all | solution.py:650
  31.2 9.1 %collective-permute-start.2 = (f32[384,128]{1,0:T(8,128)}, f32[384,128]{1,0:T(8,128)}, u32[]{:S(2)}, u32[]{:S(2)}) collective-permute-start(f32[384,128]{1,0:T(8,128)} %get-tuple-element.25), channel_id=1, source_target_pairs={{0,1},{1,0},{2,3},{3,2},{4,5},{5,4},{6,7},{7,6},{8,9},{9,8},{10,11... | collective-permute-start | bytes 589832 | tf_op jit(solution)/shard_map/ppermute | solution.py:647
  31.3 9.4 %collective-permute-start.3 = (f32[384,128]{1,0:T(8,128)}, f32[384,128]{1,0:T(8,128)}, u32[]{:S(2)}, u32[]{:S(2)}) collective-permute-start(f32[384,128]{1,0:T(8,128)} %get-tuple-element.26), channel_id=1, source_target_pairs={{1,2},{2,1},{3,4},{4,3},{5,6},{6,5},{7,8},{8,7},{9,10},{10,9},{11,... | collective-permute-start | bytes 589832 | tf_op jit(solution)/shard_map/ppermute | solution.py:647

commit v4 on v3

--- a/solution.py
+++ b/solution.py
@@ -435,8 +435,7 @@
     return rates
 
 
-def outer_rate(field, nu, inp, me, slab):
-    filtered = filtered_inner(inp, me)
+def outer_rate(filtered, field, nu, inp, me, slab):
     edge_ref, one_ref, two_ref = inp("edge"), inp("one"), inp("two")
     before_sector = (me + SECT - 1) % SECT
     after_sector = (me + 1) % SECT
@@ -503,15 +502,35 @@
     return [[[ref[block(c, z, h), :] for h in range(2)] for z in range(2)] for c in range(3)]
 
 
+def short_arrivals(edge_ref, cnt_ref, me, slab):
+    lane = lane_iota((1, CAP))
+    half = CAP // 2
+    order = [(me + k) % SECT for k in (1, SECT - 1, 2, 3, 4, 5, 6)]
+
+    def pick(get):
+        full = [get(s, lane) for s in order[:2]]
+        pairs = [
+            jnp.where(lane < half, get(order[k], lane), pltpu.roll(get(order[k + 1], lane), half, 1)) for k in (2, 4)
+        ]
+        return jnp.concatenate(full + pairs + [jnp.where(lane < half, get(order[6], lane), 0.0)], axis=1)
+
+    live = pick(lambda s, lane: (lane < cnt_ref[s, 0, me]).astype(f32))
+    values = [pick(lambda s, lane, q=q: edge_ref[s, EDGE_PART + q : EDGE_PART + q + 1, :]) for q in range(6)]
+    theta, r, z = [x.astype(i32) for x in values[3:]]
+    row = jnp.where(live > 0.5, local_row(theta, r, z, me, slab), -1)
+    return row, r % 128, values[:3]
+
+
 def first_kernel(inp, out):
     me = lax.axis_index("az")
     slab = lax.axis_index("ax")
-    live, row, col, velocity = arrivals(inp("edge"), inp("cnt"), me, slab)
-    arrived = add_parts(deposit(row, col, velocity, SECT * CAP))
+    row, col, velocity = short_arrivals(inp("edge"), inp("cnt"), me, slab)
+    arrived = add_parts(deposit(row, col, velocity, 5 * CAP))
+    filtered = filtered_inner(inp, me)
     sum_ref = inp("sums")
     total = [sum_ref[c * 256 : (c + 1) * 256, :] + arrived[c] for c in range(4)]
     nu, field = viscosity_blocks(inp, out), input_blocks(inp)
-    rates = outer_rate(field, nu, inp, me, slab)
+    rates = outer_rate(filtered, field, nu, inp, me, slab)
     local_ref = inp("local")
     mid_ref, rest_ref = out.vmem("mid"), out.vmem("rest")
     mid = [[[None, None], [None, None]] for _ in range(3)]
@@ -524,14 +543,14 @@
                 mid[c][z][h] = u1
                 mid_ref[block(c, z, h), :] = u1
                 rest_ref[block(c, z, h), :] = 0.5 * (x + u1) + DT * (0.8 * s + 0.2 * n * x - n * u1)
+    out.send("mid")
+    out.send("rest")
     write_message(out.vmem("inner"), out.vmem("edge"), mid, [nu[z][0] for z in range(2)], me)
     send_inner(out, ROW_EDGE)
     out.copy(out.vmem("edge"), out.hbm("msg").at[:, ROW_EDGE:, :])
     write_axial(out.vmem("one"), out.vmem("two"), mid, slab)
     out.send("one")
     out.send("two")
-    out.send("mid")
-    out.send("rest")
 
 
 def take(pick, row, col, n):
@@ -581,7 +600,8 @@
 def second_kernel(inp, out):
     me = lax.axis_index("az")
     slab = lax.axis_index("ax")
-    rates = outer_rate(blocks(inp("mid")), viscosity_blocks(inp, out), inp, me, slab)
+    filtered = filtered_inner(inp, me)
+    rates = outer_rate(filtered, blocks(inp("mid")), viscosity_blocks(inp, out), inp, me, slab)
     part_ref, new_ref = inp("part"), out.vmem("new")
     for c in range(3):
         for z in range(2):
@@ -715,7 +735,7 @@
     (new,) = call(
         second_kernel,
         "second_section",
-        {"inner": recv2} | tables | {"edge": recv2, "mid": mid, "nu": nu, "one": one2, "two": two2, "part": part},
+        {"edge": recv2, "inner": recv2} | tables | { "mid": mid, "nu": nu, "one": one2, "two": two2, "part": part},
         {"new": field},
         {"nu": ((256, 128), f32), "new": field},
         3,

time: 48.4 us -> 48.1 us (level)
  no operation moved by 1% of the time
where the time goes in v4:
time: 48.1 us; the launch traced here: 47.7 us
  Pallas kernels  25.3 us (53%)
  starting transfers between devices  13.8 us (29%)
  waiting for transfers between devices  7.71 us (16%)
  between operations  0.87 us (2%)
    pallas_call x5, Pallas kernels, call(): pl.pallas_call(body, out_shape=[jax.ShapeDtypeStruct(*outs[n]) for n in o...  25.3 us
    all_to_all x2, starting transfers between devices, to_all(): return lax.all_to_all(msg, 'az', split_axis=0, concat_axis=0, tiled=True)  9.54 us
    all_to_all x2, waiting for transfers between devices, to_all(): return lax.all_to_all(msg, 'az', split_axis=0, concat_axis=0, tiled=True)  7.29 us
    ppermute x2, starting transfers between devices, swap(): lax.ppermute(two, ('az', 'ax'), swap_two)  4.17 us
  transfers between devices with their start and end apart: 6, of which 3 were waited for; matrix products, arithmetic and copies ran while one was open for 0% of the time, Pallas kernels for 30%

profile of v4, /device:TPU:128, one launch (start us, length us, event | category | flops | bytes accessed | tf_op | source)
XLA Modules:
  0.0 47.7 jit_solution(8169181724046275408)
XLA Ops:
  0.6 2.7 %pack.1 = (f32[8,120,128]{2,1,0:T(8,128)}, f32[384,128]{1,0:T(8,128)}, f32[384,128]{1,0:T(8,128)}, f32[1,8192]{1,0:T(1,128)}) custom-call(f32[768,128]{1,0:T(8,128)} %bitcast.21, bf16[256,128]{1,0:T(8,128)(2,1)} %bitcast.25, s32[3,8192]{1,0:T(4,128)} %refs_2_.8, f32[3,8192]{1,0:T(4,128)} %refs_4_.4, s32[1,8,128]{2,1,0:T(8,128)} %refs_4_.3, s32[8,1,8]{2,1,0:T(1,128)} %refs_9_.1), custom_call_target="tpu_custom_call" | custom-call | bytes 2097152 | tf_op jit(solution)/shard_map/pack/pallas_call | solution.py:635
  3.3 5.4 %all-to-all-start = ((f32[8,120,128]{2,1,0:T(8,128)}), f32[8,120,128]{2,1,0:T(8,128)}, u32[]{:S(2)}, u32[]{:S(2)}) async-start(f32[8,120,128]{2,1,0:T(8,128)} %get-tuple-element.17), calls=%async_computation | async-start | bytes 983040 | tf_op jit(solution)/shard_map/all_to_all | solution.py:670
  8.7 0.0 collective-permute-start
  8.8 2.4 %collective-permute-start.1 = (f32[384,128]{1,0:T(8,128)}, f32[384,128]{1,0:T(8,128)}, u32[]{:S(2)}, u32[]{:S(2)}) collective-permute-start(f32[384,128]{1,0:T(8,128)} %get-tuple-element.21), channel_id=1, source_target_pairs={{1,2},{2,1},{3,4},{4,3},{5,6},{6,5},{7,8},{8,7},{9,10},{10,9},{11,... | collective-permute-start | bytes 589832 | tf_op jit(solution)/shard_map/ppermute | solution.py:667
  11.1 7.1 %deposit.1 = (f32[1024,128]{1,0:T(8,128)}, f32[768,128]{1,0:T(8,128)}) custom-call(s32[3,8192]{1,0:T(4,128)} %refs_2_.8, f32[1,8192]{1,0:T(1,128)} %get-tuple-element.18.refs_1_.refs_3_, f32[3,8192]{1,0:T(4,128)} %refs_4_.4, f32[768,128]{1,0:T(8,128)} %bitcast.22, bf16[256,128]{1,0:T(8,128)(2,1)} %bitcast.26, bf16[768,128]{1,0:T(8,128)(2,1)} %bitcast.31), custom_call_target="tpu_custom_call" | custom-call | flops 3758096384 | bytes 2097152 | tf_op jit(solution)/shard_map/deposit/pallas_call | solution.py:635
  18.3 0.0 collective-permute-done.refs_9_
  18.3 0.0 collective-permute-done.1.refs_10_
  18.3 3.9 %all-to-all-done.refs_0_.refs_1_.refs_8_ = f32[8,120,128]{2,1,0:T(8,128)} async-done(((f32[8,120,128]{2,1,0:T(8,128)}), f32[8,120,128]{2,1,0:T(8,128)}, u32[]{:S(2)}, u32[]{:S(2)}) %all-to-all-start) | async-done | bytes 491552 | tf_op jit(solution)/shard_map/all_to_all | solution.py:670
  22.2 4.8 %first_section.1 = (f32[8,112,128]{2,1,0:T(8,128)}, f32[384,128]{1,0:T(8,128)}, f32[384,128]{1,0:T(8,128)}, f32[768,128]{1,0:T(8,128)}, f32[768,128]{1,0:T(8,128)}) custom-call(f32[8,120,128]{2,1,0:T(8,128)} %all-to-all-done.refs_0_.refs_1_.refs_8_, f32[8,120,128]{2,1,0:T(8,128)} %all-to-all-done.refs_0_.refs_1_.refs_8_, s32[8,1,8]{2,1,0:T(1,128)} %refs_9_.1, ...), custom_call_target="tpu_custom_call" | custom-call | bytes 2097152 | tf_op jit(solution)/shard_map/first_section/pallas_call | solution.py:635
  27.0 4.1 %all-to-all-start.1 = ((f32[8,112,128]{2,1,0:T(8,128)}), f32[8,112,128]{2,1,0:T(8,128)}, u32[]{:S(2)}, u32[]{:S(2)}) async-start(f32[8,112,128]{2,1,0:T(8,128)} %get-tuple-element.23), calls=%async_computation.1 | async-start | bytes 917504 | tf_op jit(solution)/shard_map/all_to_all | solution.py:670
  31.1 0.1 collective-permute-start.2
  31.2 1.8 %collective-permute-start.3 = (f32[384,128]{1,0:T(8,128)}, f32[384,128]{1,0:T(8,128)}, u32[]{:S(2)}, u32[]{:S(2)}) collective-permute-start(f32[384,128]{1,0:T(8,128)} %get-tuple-element.26), channel_id=1, source_target_pairs={{1,2},{2,1},{3,4},{4,3},{5,6},{6,5},{7,8},{8,7},{9,10},{10,9},{11,... | collective-permute-start | bytes 589832 | tf_op jit(solution)/shard_map/ppermute | solution.py:667
  33.0 7.2 %take.1 = (f32[3,8192]{1,0:T(4,128)}, f32[3,1,1024]{2,1,0:T(1,128)}, f32[768,128]{1,0:T(8,128)}) custom-call(f32[768,128]{1,0:T(8,128)} %bitcast.24, f32[768,128]{1,0:T(8,128)} %get-tuple-element.24.refs_1_.refs_5_, s32[3,8192]{1,0:T(4,128)} %refs_2_.8, f32[1,8192]{1,0:T(1,128)} %get-tuple-element.18.refs_1_.refs_3_, f32[3,8192]{1,0:T(4,128)} %refs_4_.4, ...), custom_call_target="tpu_custom_call" | custom-call | flops 3221225472 | bytes 2097152 | tf_op jit(solution)/shard_map/take/pallas_call | solution.py:635
  40.2 0.0 collective-permute-done.2.refs_7_
  40.2 0.4 collective-permute-done.3.refs_8_
  40.6 3.4 %all-to-all-done.1.refs_0_.refs_1_ = f32[8,112,128]{2,1,0:T(8,128)} async-done(((f32[8,112,128]{2,1,0:T(8,128)}), f32[8,112,128]{2,1,0:T(8,128)}, u32[]{:S(2)}, u32[]{:S(2)}) %all-to-all-start.1) | async-done | bytes 458784 | tf_op jit(solution)/shard_map/all_to_all | solution.py:670
  44.1 3.5 %second_section.1 = f32[768,128]{1,0:T(8,128)} custom-call(f32[8,112,128]{2,1,0:T(8,128)} %all-to-all-done.1.refs_0_.refs_1_, f32[8,112,128]{2,1,0:T(8,128)} %all-to-all-done.1.refs_0_.refs_1_, f32[2,256,256]{2,1,0:T(8,128)} %constant.6.clone.refs_3_.refs_2_, f32[2,256,128]{2,1,0:T(8,128)} %constant.7.clone.refs_7_.refs_3_, ...), custom_call_target="tpu_custom_call" | custom-call | bytes 2097152 | tf_op jit(solution)/shard_map/second_section/pallas_call | solution.py:635
Async XLA Ops:
  3.3 18.8 %all-to-all-start = ((f32[8,120,128]{2,1,0:T(8,128)}), f32[8,120,128]{2,1,0:T(8,128)}, u32[]{:S(2)}, u32[]{:S(2)}) async-start(f32[8,120,128]{2,1,0:T(8,128)} %get-tuple-element.17), calls=%async_computation | async-start | bytes 983040 | tf_op jit(solution)/shard_map/all_to_all | solution.py:670
  8.7 9.5 %collective-permute-start = (f32[384,128]{1,0:T(8,128)}, f32[384,128]{1,0:T(8,128)}, u32[]{:S(2)}, u32[]{:S(2)}) collective-permute-start(f32[384,128]{1,0:T(8,128)} %get-tuple-element.20), channel_id=1, source_target_pairs={{0,1},{1,0},{2,3},{3,2},{4,5},{5,4},{6,7},{7,6},{8,9},{9,8},{10,11... | collective-permute-start | bytes 589832 | tf_op jit(solution)/shard_map/ppermute | solution.py:667
  8.8 9.5 %collective-permute-start.1 = (f32[384,128]{1,0:T(8,128)}, f32[384,128]{1,0:T(8,128)}, u32[]{:S(2)}, u32[]{:S(2)}) collective-permute-start(f32[384,128]{1,0:T(8,128)} %get-tuple-element.21), channel_id=1, source_target_pairs={{1,2},{2,1},{3,4},{4,3},{5,6},{6,5},{7,8},{8,7},{9,10},{10,9},{11,... | collective-permute-start | bytes 589832 | tf_op jit(solution)/shard_map/ppermute | solution.py:667
  27.0 17.1 %all-to-all-start.1 = ((f32[8,112,128]{2,1,0:T(8,128)}), f32[8,112,128]{2,1,0:T(8,128)}, u32[]{:S(2)}, u32[]{:S(2)}) async-start(f32[8,112,128]{2,1,0:T(8,128)} %get-tuple-element.23), calls=%async_computation.1 | async-start | bytes 917504 | tf_op jit(solution)/shard_map/all_to_all | solution.py:670
  31.1 9.1 %collective-permute-start.2 = (f32[384,128]{1,0:T(8,128)}, f32[384,128]{1,0:T(8,128)}, u32[]{:S(2)}, u32[]{:S(2)}) collective-permute-start(f32[384,128]{1,0:T(8,128)} %get-tuple-element.25), channel_id=1, source_target_pairs={{0,1},{1,0},{2,3},{3,2},{4,5},{5,4},{6,7},{7,6},{8,9},{9,8},{10,11... | collective-permute-start | bytes 589832 | tf_op jit(solution)/shard_map/ppermute | solution.py:667
  31.2 9.4 %collective-permute-start.3 = (f32[384,128]{1,0:T(8,128)}, f32[384,128]{1,0:T(8,128)}, u32[]{:S(2)}, u32[]{:S(2)}) collective-permute-start(f32[384,128]{1,0:T(8,128)} %get-tuple-element.26), channel_id=1, source_target_pairs={{1,2},{2,1},{3,4},{4,3},{5,6},{6,5},{7,8},{8,7},{9,10},{10,9},{11,... | collective-permute-start | bytes 589832 | tf_op jit(solution)/shard_map/ppermute | solution.py:667

commit v5 on v4

--- a/solution.py
+++ b/solution.py
@@ -208,7 +208,7 @@
 
 def pack_kernel(inp, out):
     me = lax.axis_index("az")
-    tmp_ref, nu_s, edge_ref, stay_ref = out.vmem("tmp"), out.vmem("nu"), out.vmem("edge"), out.vmem("stay")
+    tmp_ref, nu_s, edge_ref = out.vmem("tmp"), out.vmem("nu"), out.vmem("edge")
     vel_ref, nu_ref = inp("vel"), inp("nu")
     field = [[[vel_ref[strided(c, z, h), :] for h in range(2)] for z in range(2)] for c in range(3)]
     nu_s[...] = nu_ref[...].astype(f32)
@@ -226,15 +226,10 @@
     for k in range(2):
         for c in range(3):
             parts.append(jnp.concatenate(split2(tmp_ref[pl.ds(k * 512 + c, 64, stride=8), :]), axis=1))
-    rows_ref, cnt_ref = inp("rows"), inp("cnt")
-    lane = lane_iota((1, 128))
+    rows_ref = inp("rows")
     listed = [rows_ref[0, t : t + 1, :] for t in range(SECT)]
     low = jnp.concatenate([one_hot(row % 128, 128, 128) for row in listed], axis=1)
     high = [row_iota((64, 128)) == row // 128 for row in listed]
-    used_high = []
-    for t in range(SECT):
-        used = (high[t] & (lane < cnt_ref[me, 0, t])).astype(f32)
-        used_high.append(used.astype(bf16))
     picked = jnp.dot(
         jnp.concatenate(parts, axis=0), jnp.concatenate([low, low], axis=0), preferred_element_type=f32
     )
@@ -245,13 +240,6 @@
                 jnp.where(high[t], value, 0.0), axis=0, keepdims=True
             )
     out.copy(edge_ref, out.hbm("msg").at[:, ROW_EDGE:, :])
-    leaving = lax.dot_general(
-        jnp.concatenate(used_high, axis=1), low, (((1,), (1,)), ((), ())), preferred_element_type=f32
-    )
-    stay = 1.0 - leaving
-    for i in range(64):
-        stay_ref[0:1, i * 128 : (i + 1) * 128] = stay[i : i + 1, :]
-    out.send("stay")
 
 
 def local_row(theta, r, z, me, slab):
@@ -296,10 +284,32 @@
                 ref[block(c, z, h), :] = x[c][z][h]
 
 
+def write_stay(stay_ref, rows_ref, cnt_ref, me):
+    lane = lane_iota((1, 128))
+    lows, highs = [], []
+    for t in range(SECT):
+        row = rows_ref[0, t : t + 1, :]
+        used = (row_iota((64, 128)) == row // 128) & (lane < cnt_ref[me, 0, t])
+        highs.append(used.astype(f32).astype(bf16))
+        lows.append(one_hot(row % 128, 128, 128))
+    leaving = lax.dot_general(
+        jnp.concatenate(highs, axis=1),
+        jnp.concatenate(lows, axis=1),
+        (((1,), (1,)), ((), ())),
+        preferred_element_type=f32,
+    )
+    stay = 1.0 - leaving
+    for i in range(64):
+        stay_ref[0:1, i * 128 : (i + 1) * 128] = stay[i : i + 1, :]
+
+
 def scatter_kernel(inp, out):
     me = lax.axis_index("az")
     slab = lax.axis_index("ax")
-    pc_ref, stay_ref, pv_ref = inp("pc"), inp("stay"), inp("pv")
+    stay_ref = out.vmem("stay")
+    write_stay(stay_ref, inp("rows"), inp("cnt"), me)
+    out.send("stay")
+    pc_ref, pv_ref = inp("pc"), inp("pv")
     sum_ref, acc_ref = out.vmem("sums"), out.vmem("acc")
     for k in range(NP // CHUNK):
         part = pl.ds(k * CHUNK, CHUNK)
@@ -672,33 +682,32 @@
     face = ((384, 128), f32)
     field = ((768, 128), f32)
     materials = {"nu": ((256, 128), f32), "mag": field}
-    msg, one, two, stay = call(
+    msg, one, two = call(
         pack_kernel,
         "pack",
-        {"vel": vel, "nu": nu, "pc": pc, "pv": pv, "rows": send_rows, "cnt": send_counts},
-        {"msg": ((SECT, ROW_EDGE + EDGE1, 128), f32), "one": face, "two": face, "stay": ((1, NP), f32)},
+        {"vel": vel, "nu": nu, "pc": pc, "pv": pv, "rows": send_rows},
+        {"msg": ((SECT, ROW_EDGE + EDGE1, 128), f32), "one": face, "two": face},
         {
             "inner": ((ROW_EDGE, 128), f32),
             "one": face,
             "two": face,
             "edge": ((SECT, EDGE1, 128), f32),
-            "stay": ((1, NP), f32),
             "tmp": ((1024, 128), f32),
             "nu": ((256, 128), f32),
         },
-        12,
-        in_smem=("cnt",),
+        11,
     )
     one, two = swap(one, two)
     recv = to_all(msg)
-    sums, local = call(
+    sums, local, stay = call(
         scatter_kernel,
         "deposit",
-        {"pc": pc, "stay": stay, "pv": pv, "vel": vel, "nu": nu, "mag": mag},
-        {"sums": ((1024, 128), f32), "local": field},
-        {"sums": ((1024, 128), f32), "acc": ((256, 896), f32), "local": field} | materials,
-        2,
+        {"rows": send_rows, "cnt": send_counts, "pc": pc, "pv": pv, "vel": vel, "nu": nu, "mag": mag},
+        {"sums": ((1024, 128), f32), "local": field, "stay": ((1, NP), f32)},
+        {"sums": ((1024, 128), f32), "acc": ((256, 896), f32), "local": field, "stay": ((1, NP), f32)} | materials,
+        3,
         flops=2 * NP * 256 * 896,
+        in_smem=("cnt",),
     )
     msg2, one2, two2, mid, rest = call(
         first_kernel,

time: 48.1 us -> 47.9 us (level)
  transfers between devices with their start and end apart: 6 -> 6, of which waited for: 3 -> 3; matrix products, arithmetic and copies ran while one was open for 0% -> 0% of each run, Pallas kernels for 30% -> 31%
where the time goes in v5:
time: 47.9 us; the launch traced here: 47.6 us
  Pallas kernels  25.5 us (53%)
  starting transfers between devices  13.8 us (29%)
  waiting for transfers between devices  7.45 us (16%)
  between operations  0.87 us (2%)
    pallas_call x5, Pallas kernels, call(): pl.pallas_call(body, out_shape=[jax.ShapeDtypeStruct(*outs[n]) for n in o...  25.5 us
    all_to_all x2, starting transfers between devices, to_all(): return lax.all_to_all(msg, 'az', split_axis=0, concat_axis=0, tiled=True)  9.54 us
    all_to_all x2, waiting for transfers between devices, to_all(): return lax.all_to_all(msg, 'az', split_axis=0, concat_axis=0, tiled=True)  7.04 us
    ppermute x2, starting transfers between devices, swap(): lax.ppermute(two, ('az', 'ax'), swap_two)  4.16 us
  transfers between devices with their start and end apart: 6, of which 3 were waited for; matrix products, arithmetic and copies ran while one was open for 0% of the time, Pallas kernels for 31%

profile of v5, /device:TPU:128, one launch (start us, length us, event | category | flops | bytes accessed | tf_op | source)
XLA Modules:
  0.0 47.6 jit_solution(3916382595721358204)
XLA Ops:
  0.6 2.6 %pack.1 = (f32[8,120,128]{2,1,0:T(8,128)}, f32[384,128]{1,0:T(8,128)}, f32[384,128]{1,0:T(8,128)}) custom-call(f32[768,128]{1,0:T(8,128)} %bitcast.21, bf16[256,128]{1,0:T(8,128)(2,1)} %bitcast.25, s32[3,8192]{1,0:T(4,128)} %refs_2_.8, f32[3,8192]{1,0:T(4,128)} %refs_4_.4, s32[1,8,128]{2,1,0:T(8,128)} %refs_0_.1), custom_call_target="tpu_custom_call" | custom-call | bytes 2097152 | tf_op jit(solution)/shard_map/pack/pallas_call | solution.py:645
  3.2 5.4 %all-to-all-start = ((f32[8,120,128]{2,1,0:T(8,128)}), f32[8,120,128]{2,1,0:T(8,128)}, u32[]{:S(2)}, u32[]{:S(2)}) async-start(f32[8,120,128]{2,1,0:T(8,128)} %get-tuple-element.17), calls=%async_computation | async-start | bytes 983040 | tf_op jit(solution)/shard_map/all_to_all | solution.py:680
  8.6 0.0 collective-permute-start
  8.6 2.4 %collective-permute-start.1 = (f32[384,128]{1,0:T(8,128)}, f32[384,128]{1,0:T(8,128)}, u32[]{:S(2)}, u32[]{:S(2)}) collective-permute-start(f32[384,128]{1,0:T(8,128)} %get-tuple-element.20), channel_id=1, source_target_pairs={{1,2},{2,1},{3,4},{4,3},{5,6},{6,5},{7,8},{8,7},{9,10},{10,9},{11,... | collective-permute-start | bytes 589832 | tf_op jit(solution)/shard_map/ppermute | solution.py:677
  11.0 7.4 %deposit.1 = (f32[1024,128]{1,0:T(8,128)}, f32[768,128]{1,0:T(8,128)}, f32[1,8192]{1,0:T(1,128)}) custom-call(s32[1,8,128]{2,1,0:T(8,128)} %refs_0_.1, s32[8,1,8]{2,1,0:T(1,128)} %refs_9_.1, s32[3,8192]{1,0:T(4,128)} %refs_2_.8, f32[3,8192]{1,0:T(4,128)} %refs_4_.4, f32[768,128]{1,0:T(8,128)} %bitcast.22, bf16[256,128]{1,0:T(8,128)(2,1)} %bitcast.26, ...), custom_call_target="tpu_custom_call" | custom-call | flops 3758096384 | bytes 2097152 | tf_op jit(solution)/shard_map/deposit/pallas_call | solution.py:645
  18.4 0.0 collective-permute-done.refs_9_
  18.4 0.0 collective-permute-done.1.refs_10_
  18.4 3.6 %all-to-all-done.refs_0_.refs_1_.refs_8_ = f32[8,120,128]{2,1,0:T(8,128)} async-done(((f32[8,120,128]{2,1,0:T(8,128)}), f32[8,120,128]{2,1,0:T(8,128)}, u32[]{:S(2)}, u32[]{:S(2)}) %all-to-all-start) | async-done | bytes 491552 | tf_op jit(solution)/shard_map/all_to_all | solution.py:680
  22.0 4.8 %first_section.1 = (f32[8,112,128]{2,1,0:T(8,128)}, f32[384,128]{1,0:T(8,128)}, f32[384,128]{1,0:T(8,128)}, f32[768,128]{1,0:T(8,128)}, f32[768,128]{1,0:T(8,128)}) custom-call(f32[8,120,128]{2,1,0:T(8,128)} %all-to-all-done.refs_0_.refs_1_.refs_8_, f32[8,120,128]{2,1,0:T(8,128)} %all-to-all-done.refs_0_.refs_1_.refs_8_, s32[8,1,8]{2,1,0:T(1,128)} %refs_9_.1, ...), custom_call_target="tpu_custom_call" | custom-call | bytes 2097152 | tf_op jit(solution)/shard_map/first_section/pallas_call | solution.py:645
  26.9 4.1 %all-to-all-start.1 = ((f32[8,112,128]{2,1,0:T(8,128)}), f32[8,112,128]{2,1,0:T(8,128)}, u32[]{:S(2)}, u32[]{:S(2)}) async-start(f32[8,112,128]{2,1,0:T(8,128)} %get-tuple-element.22), calls=%async_computation.1 | async-start | bytes 917504 | tf_op jit(solution)/shard_map/all_to_all | solution.py:680
  31.0 0.1 collective-permute-start.2
  31.1 1.8 %collective-permute-start.3 = (f32[384,128]{1,0:T(8,128)}, f32[384,128]{1,0:T(8,128)}, u32[]{:S(2)}, u32[]{:S(2)}) collective-permute-start(f32[384,128]{1,0:T(8,128)} %get-tuple-element.25), channel_id=1, source_target_pairs={{1,2},{2,1},{3,4},{4,3},{5,6},{6,5},{7,8},{8,7},{9,10},{10,9},{11,... | collective-permute-start | bytes 589832 | tf_op jit(solution)/shard_map/ppermute | solution.py:677
  32.9 7.2 %take.1 = (f32[3,8192]{1,0:T(4,128)}, f32[3,1,1024]{2,1,0:T(1,128)}, f32[768,128]{1,0:T(8,128)}) custom-call(f32[768,128]{1,0:T(8,128)} %bitcast.24, f32[768,128]{1,0:T(8,128)} %get-tuple-element.23.refs_1_.refs_5_, s32[3,8192]{1,0:T(4,128)} %refs_2_.8, f32[1,8192]{1,0:T(1,128)} %get-tuple-element.26.refs_3_, f32[3,8192]{1,0:T(4,128)} %refs_4_.4, ...), custom_call_target="tpu_custom_call" | custom-call | flops 3221225472 | bytes 2097152 | tf_op jit(solution)/shard_map/take/pallas_call | solution.py:645
  40.1 0.0 collective-permute-done.2.refs_7_
  40.1 0.4 collective-permute-done.3.refs_8_
  40.5 3.4 %all-to-all-done.1.refs_0_.refs_1_ = f32[8,112,128]{2,1,0:T(8,128)} async-done(((f32[8,112,128]{2,1,0:T(8,128)}), f32[8,112,128]{2,1,0:T(8,128)}, u32[]{:S(2)}, u32[]{:S(2)}) %all-to-all-start.1) | async-done | bytes 458784 | tf_op jit(solution)/shard_map/all_to_all | solution.py:680
  43.9 3.5 %second_section.1 = f32[768,128]{1,0:T(8,128)} custom-call(f32[8,112,128]{2,1,0:T(8,128)} %all-to-all-done.1.refs_0_.refs_1_, f32[8,112,128]{2,1,0:T(8,128)} %all-to-all-done.1.refs_0_.refs_1_, f32[2,256,256]{2,1,0:T(8,128)} %constant.6.clone.refs_3_.refs_2_, f32[2,256,128]{2,1,0:T(8,128)} %constant.7.clone.refs_7_.refs_3_, ...), custom_call_target="tpu_custom_call" | custom-call | bytes 2097152 | tf_op jit(solution)/shard_map/second_section/pallas_call | solution.py:645
Async XLA Ops:
  3.2 18.8 %all-to-all-start = ((f32[8,120,128]{2,1,0:T(8,128)}), f32[8,120,128]{2,1,0:T(8,128)}, u32[]{:S(2)}, u32[]{:S(2)}) async-start(f32[8,120,128]{2,1,0:T(8,128)} %get-tuple-element.17), calls=%async_computation | async-start | bytes 983040 | tf_op jit(solution)/shard_map/all_to_all | solution.py:680
  8.6 9.8 %collective-permute-start = (f32[384,128]{1,0:T(8,128)}, f32[384,128]{1,0:T(8,128)}, u32[]{:S(2)}, u32[]{:S(2)}) collective-permute-start(f32[384,128]{1,0:T(8,128)} %get-tuple-element.19), channel_id=1, source_target_pairs={{0,1},{1,0},{2,3},{3,2},{4,5},{5,4},{6,7},{7,6},{8,9},{9,8},{10,11... | collective-permute-start | bytes 589832 | tf_op jit(solution)/shard_map/ppermute | solution.py:677
  8.6 9.8 %collective-permute-start.1 = (f32[384,128]{1,0:T(8,128)}, f32[384,128]{1,0:T(8,128)}, u32[]{:S(2)}, u32[]{:S(2)}) collective-permute-start(f32[384,128]{1,0:T(8,128)} %get-tuple-element.20), channel_id=1, source_target_pairs={{1,2},{2,1},{3,4},{4,3},{5,6},{6,5},{7,8},{8,7},{9,10},{10,9},{11,... | collective-permute-start | bytes 589832 | tf_op jit(solution)/shard_map/ppermute | solution.py:677
  26.9 17.1 %all-to-all-start.1 = ((f32[8,112,128]{2,1,0:T(8,128)}), f32[8,112,128]{2,1,0:T(8,128)}, u32[]{:S(2)}, u32[]{:S(2)}) async-start(f32[8,112,128]{2,1,0:T(8,128)} %get-tuple-element.22), calls=%async_computation.1 | async-start | bytes 917504 | tf_op jit(solution)/shard_map/all_to_all | solution.py:680
  31.0 9.1 %collective-permute-start.2 = (f32[384,128]{1,0:T(8,128)}, f32[384,128]{1,0:T(8,128)}, u32[]{:S(2)}, u32[]{:S(2)}) collective-permute-start(f32[384,128]{1,0:T(8,128)} %get-tuple-element.24), channel_id=1, source_target_pairs={{0,1},{1,0},{2,3},{3,2},{4,5},{5,4},{6,7},{7,6},{8,9},{9,8},{10,11... | collective-permute-start | bytes 589832 | tf_op jit(solution)/shard_map/ppermute | solution.py:677
  31.1 9.4 %collective-permute-start.3 = (f32[384,128]{1,0:T(8,128)}, f32[384,128]{1,0:T(8,128)}, u32[]{:S(2)}, u32[]{:S(2)}) collective-permute-start(f32[384,128]{1,0:T(8,128)} %get-tuple-element.25), channel_id=1, source_target_pairs={{1,2},{2,1},{3,4},{4,3},{5,6},{6,5},{7,8},{8,7},{9,10},{10,9},{11,... | collective-permute-start | bytes 589832 | tf_op jit(solution)/shard_map/ppermute | solution.py:677

commit v6 on v5

--- a/solution.py
+++ b/solution.py
@@ -2,6 +2,7 @@
 
 import jax
 import jax.numpy as jnp
+import ml_dtypes
 import numpy as np
 from jax import lax
 from jax.experimental import pallas as pl
@@ -18,7 +19,6 @@
 DTHETA = 2.0 * math.pi / NA
 DT = 0.02
 POLE_SIGNS = (-1.0, -1.0, 1.0)
-HIGHEST = lax.Precision.HIGHEST
 f32 = jnp.float32
 bf16 = jnp.bfloat16
 i32 = jnp.int32
@@ -31,6 +31,14 @@
 EDGE1 = 24
 EDGE2 = 16
 CHUNK = 1024
+
+
+def table_parts(x):
+    parts = []
+    for _ in range(3):
+        parts.append(x.astype(ml_dtypes.bfloat16))
+        x = x - parts[-1].astype(np.float32)
+    return np.concatenate(parts, axis=-1)
 
 
 def filter_tables():
@@ -50,7 +58,7 @@
     cutoff = 4.0 * (np.arange(KR) + 0.5)
     weight = 1.0 / (1.0 + (modes[:, :, None] / cutoff) ** 4)
     weight = np.tile(weight, (1, 1, 128 // KR)).astype(np.float32)
-    return basis, np.ascontiguousarray(basis.transpose(0, 2, 1)), weight
+    return table_parts(basis), table_parts(basis.transpose(0, 2, 1)), weight
 
 
 BASIS, BASIS_T, MODE_WEIGHT = filter_tables()
@@ -371,16 +379,29 @@
     return jnp.concatenate(out[0], axis=0), jnp.concatenate(out[1], axis=0)
 
 
+def table_dot(table, x):
+    q = [table[:, k * 256 : (k + 1) * 256] for k in range(3)]
+    hi = x.astype(bf16)
+    rest = x - hi.astype(f32)
+    mid = rest.astype(bf16)
+    low = (rest - mid.astype(f32)).astype(bf16)
+    return jnp.dot(
+        jnp.concatenate([q[2], q[1], q[0], q[1], q[0], q[0]], axis=1),
+        jnp.concatenate([hi, mid, low, hi, mid, hi], axis=0),
+        preferred_element_type=f32,
+    )
+
+
 def filtered_inner(inp, me):
     part = jnp.concatenate(whole_azimuth_part(inp), axis=1)
     low, high = part[: NA // 2], part[NA // 2 :]
     basis_ref, weight_ref, basis_t_ref = inp("basis"), inp("weight"), inp("basis_t")
     out = 0.0
     for parity, x in enumerate((low + high, low - high)):
-        spectrum = jnp.dot(basis_ref[parity], x, precision=HIGHEST, preferred_element_type=f32)
+        spectrum = table_dot(basis_ref[parity], x)
         weight = weight_ref[parity]
         spectrum = spectrum * jnp.concatenate([weight, weight], axis=1)
-        back = jnp.dot(basis_t_ref[parity], spectrum, precision=HIGHEST, preferred_element_type=f32)
+        back = table_dot(basis_t_ref[parity], spectrum)
         if parity:
             back = jnp.where(me < 4, back, -back)
         out = out + back

time: 47.9 us -> 47.9 us (level)
  no operation moved by 1% of the time
where the time goes in v6:
time: 47.9 us; the launch traced here: 47.6 us
  Pallas kernels  25.4 us (53%)
  starting transfers between devices  13.8 us (29%)
  waiting for transfers between devices  7.46 us (16%)
  between operations  0.87 us (2%)
    pallas_call x5, Pallas kernels, call(): pl.pallas_call(body, out_shape=[jax.ShapeDtypeStruct(*outs[n]) for n in o...  25.4 us
    all_to_all x2, starting transfers between devices, to_all(): return lax.all_to_all(msg, 'az', split_axis=0, concat_axis=0, tiled=True)  9.54 us
    all_to_all x2, waiting for transfers between devices, to_all(): return lax.all_to_all(msg, 'az', split_axis=0, concat_axis=0, tiled=True)  7.04 us
    ppermute x2, starting transfers between devices, swap(): lax.ppermute(two, ('az', 'ax'), swap_two)  4.16 us
  transfers between devices with their start and end apart: 6, of which 3 were waited for; matrix products, arithmetic and copies ran while one was open for 0% of the time, Pallas kernels for 31%

profile of v6, /device:TPU:128, one launch (start us, length us, event | category | flops | bytes accessed | tf_op | source)
XLA Modules:
  0.0 47.6 jit_solution(1879248017548726664)
XLA Ops:
  0.6 2.6 %pack.1 = (f32[8,120,128]{2,1,0:T(8,128)}, f32[384,128]{1,0:T(8,128)}, f32[384,128]{1,0:T(8,128)}) custom-call(f32[768,128]{1,0:T(8,128)} %bitcast.21, bf16[256,128]{1,0:T(8,128)(2,1)} %bitcast.25, s32[3,8192]{1,0:T(4,128)} %refs_2_.8, f32[3,8192]{1,0:T(4,128)} %refs_4_.4, s32[1,8,128]{2,1,0:T(8,128)} %refs_0_.1), custom_call_target="tpu_custom_call" | custom-call | bytes 2097152 | tf_op jit(solution)/shard_map/pack/pallas_call | solution.py:666
  3.2 5.4 %all-to-all-start = ((f32[8,120,128]{2,1,0:T(8,128)}), f32[8,120,128]{2,1,0:T(8,128)}, u32[]{:S(2)}, u32[]{:S(2)}) async-start(f32[8,120,128]{2,1,0:T(8,128)} %get-tuple-element.17), calls=%async_computation | async-start | bytes 983040 | tf_op jit(solution)/shard_map/all_to_all | solution.py:701
  8.6 0.0 collective-permute-start
  8.6 2.4 %collective-permute-start.1 = (f32[384,128]{1,0:T(8,128)}, f32[384,128]{1,0:T(8,128)}, u32[]{:S(2)}, u32[]{:S(2)}) collective-permute-start(f32[384,128]{1,0:T(8,128)} %get-tuple-element.20), channel_id=1, source_target_pairs={{1,2},{2,1},{3,4},{4,3},{5,6},{6,5},{7,8},{8,7},{9,10},{10,9},{11,... | collective-permute-start | bytes 589832 | tf_op jit(solution)/shard_map/ppermute | solution.py:698
  11.0 7.4 %deposit.1 = (f32[1024,128]{1,0:T(8,128)}, f32[768,128]{1,0:T(8,128)}, f32[1,8192]{1,0:T(1,128)}) custom-call(s32[1,8,128]{2,1,0:T(8,128)} %refs_0_.1, s32[8,1,8]{2,1,0:T(1,128)} %refs_9_.1, s32[3,8192]{1,0:T(4,128)} %refs_2_.8, f32[3,8192]{1,0:T(4,128)} %refs_4_.4, f32[768,128]{1,0:T(8,128)} %bitcast.22, bf16[256,128]{1,0:T(8,128)(2,1)} %bitcast.26, ...), custom_call_target="tpu_custom_call" | custom-call | flops 3758096384 | bytes 2097152 | tf_op jit(solution)/shard_map/deposit/pallas_call | solution.py:666
  18.4 0.0 collective-permute-done.refs_9_
  18.4 0.0 collective-permute-done.1.refs_10_
  18.4 3.6 %all-to-all-done.refs_0_.refs_1_.refs_8_ = f32[8,120,128]{2,1,0:T(8,128)} async-done(((f32[8,120,128]{2,1,0:T(8,128)}), f32[8,120,128]{2,1,0:T(8,128)}, u32[]{:S(2)}, u32[]{:S(2)}) %all-to-all-start) | async-done | bytes 491552 | tf_op jit(solution)/shard_map/all_to_all | solution.py:701
  22.0 4.8 %first_section.1 = (f32[8,112,128]{2,1,0:T(8,128)}, f32[384,128]{1,0:T(8,128)}, f32[384,128]{1,0:T(8,128)}, f32[768,128]{1,0:T(8,128)}, f32[768,128]{1,0:T(8,128)}) custom-call(f32[8,120,128]{2,1,0:T(8,128)} %all-to-all-done.refs_0_.refs_1_.refs_8_, f32[8,120,128]{2,1,0:T(8,128)} %all-to-all-done.refs_0_.refs_1_.refs_8_, s32[8,1,8]{2,1,0:T(1,128)} %refs_9_.1, ...), custom_call_target="tpu_custom_call" | custom-call | bytes 2097152 | tf_op jit(solution)/shard_map/first_section/pallas_call | solution.py:666
  26.8 4.1 %all-to-all-start.1 = ((f32[8,112,128]{2,1,0:T(8,128)}), f32[8,112,128]{2,1,0:T(8,128)}, u32[]{:S(2)}, u32[]{:S(2)}) async-start(f32[8,112,128]{2,1,0:T(8,128)} %get-tuple-element.22), calls=%async_computation.1 | async-start | bytes 917504 | tf_op jit(solution)/shard_map/all_to_all | solution.py:701
  31.0 0.1 collective-permute-start.2
  31.1 1.8 %collective-permute-start.3 = (f32[384,128]{1,0:T(8,128)}, f32[384,128]{1,0:T(8,128)}, u32[]{:S(2)}, u32[]{:S(2)}) collective-permute-start(f32[384,128]{1,0:T(8,128)} %get-tuple-element.25), channel_id=1, source_target_pairs={{1,2},{2,1},{3,4},{4,3},{5,6},{6,5},{7,8},{8,7},{9,10},{10,9},{11,... | collective-permute-start | bytes 589832 | tf_op jit(solution)/shard_map/ppermute | solution.py:698
  32.8 7.2 %take.1 = (f32[3,8192]{1,0:T(4,128)}, f32[3,1,1024]{2,1,0:T(1,128)}, f32[768,128]{1,0:T(8,128)}) custom-call(f32[768,128]{1,0:T(8,128)} %bitcast.24, f32[768,128]{1,0:T(8,128)} %get-tuple-element.23.refs_1_.refs_5_, s32[3,8192]{1,0:T(4,128)} %refs_2_.8, f32[1,8192]{1,0:T(1,128)} %get-tuple-element.26.refs_3_, f32[3,8192]{1,0:T(4,128)} %refs_4_.4, ...), custom_call_target="tpu_custom_call" | custom-call | flops 3221225472 | bytes 2097152 | tf_op jit(solution)/shard_map/take/pallas_call | solution.py:666
  40.0 0.0 collective-permute-done.2.refs_7_
  40.0 0.4 collective-permute-done.3.refs_8_
  40.5 3.4 %all-to-all-done.1.refs_0_.refs_1_ = f32[8,112,128]{2,1,0:T(8,128)} async-done(((f32[8,112,128]{2,1,0:T(8,128)}), f32[8,112,128]{2,1,0:T(8,128)}, u32[]{:S(2)}, u32[]{:S(2)}) %all-to-all-start.1) | async-done | bytes 458784 | tf_op jit(solution)/shard_map/all_to_all | solution.py:701
  43.9 3.5 %second_section.1 = f32[768,128]{1,0:T(8,128)} custom-call(f32[8,112,128]{2,1,0:T(8,128)} %all-to-all-done.1.refs_0_.refs_1_, f32[8,112,128]{2,1,0:T(8,128)} %all-to-all-done.1.refs_0_.refs_1_, bf16[2,256,768]{2,1,0:T(8,128)(2,1)} %constant.6.clone.refs_3_.refs_2_, f32[2,256,128]{2,1,0:T(8,128)} %constant.7.clone.refs_7_.refs_3_, ...), custom_call_target="tpu_custom_call" | custom-call | bytes 2097152 | tf_op jit(solution)/shard_map/second_section/pallas_call | solution.py:666
Async XLA Ops:
  3.2 18.8 %all-to-all-start = ((f32[8,120,128]{2,1,0:T(8,128)}), f32[8,120,128]{2,1,0:T(8,128)}, u32[]{:S(2)}, u32[]{:S(2)}) async-start(f32[8,120,128]{2,1,0:T(8,128)} %get-tuple-element.17), calls=%async_computation | async-start | bytes 983040 | tf_op jit(solution)/shard_map/all_to_all | solution.py:701
  8.6 9.8 %collective-permute-start = (f32[384,128]{1,0:T(8,128)}, f32[384,128]{1,0:T(8,128)}, u32[]{:S(2)}, u32[]{:S(2)}) collective-permute-start(f32[384,128]{1,0:T(8,128)} %get-tuple-element.19), channel_id=1, source_target_pairs={{0,1},{1,0},{2,3},{3,2},{4,5},{5,4},{6,7},{7,6},{8,9},{9,8},{10,11... | collective-permute-start | bytes 589832 | tf_op jit(solution)/shard_map/ppermute | solution.py:698
  8.6 9.8 %collective-permute-start.1 = (f32[384,128]{1,0:T(8,128)}, f32[384,128]{1,0:T(8,128)}, u32[]{:S(2)}, u32[]{:S(2)}) collective-permute-start(f32[384,128]{1,0:T(8,128)} %get-tuple-element.20), channel_id=1, source_target_pairs={{1,2},{2,1},{3,4},{4,3},{5,6},{6,5},{7,8},{8,7},{9,10},{10,9},{11,... | collective-permute-start | bytes 589832 | tf_op jit(solution)/shard_map/ppermute | solution.py:698
  26.8 17.1 %all-to-all-start.1 = ((f32[8,112,128]{2,1,0:T(8,128)}), f32[8,112,128]{2,1,0:T(8,128)}, u32[]{:S(2)}, u32[]{:S(2)}) async-start(f32[8,112,128]{2,1,0:T(8,128)} %get-tuple-element.22), calls=%async_computation.1 | async-start | bytes 917504 | tf_op jit(solution)/shard_map/all_to_all | solution.py:701
  31.0 9.1 %collective-permute-start.2 = (f32[384,128]{1,0:T(8,128)}, f32[384,128]{1,0:T(8,128)}, u32[]{:S(2)}, u32[]{:S(2)}) collective-permute-start(f32[384,128]{1,0:T(8,128)} %get-tuple-element.24), channel_id=1, source_target_pairs={{0,1},{1,0},{2,3},{3,2},{4,5},{5,4},{6,7},{7,6},{8,9},{9,8},{10,11... | collective-permute-start | bytes 589832 | tf_op jit(solution)/shard_map/ppermute | solution.py:698
  31.1 9.4 %collective-permute-start.3 = (f32[384,128]{1,0:T(8,128)}, f32[384,128]{1,0:T(8,128)}, u32[]{:S(2)}, u32[]{:S(2)}) collective-permute-start(f32[384,128]{1,0:T(8,128)} %get-tuple-element.25), channel_id=1, source_target_pairs={{1,2},{2,1},{3,4},{4,3},{5,6},{6,5},{7,8},{8,7},{9,10},{10,9},{11,... | collective-permute-start | bytes 589832 | tf_op jit(solution)/shard_map/ppermute | solution.py:698
